TPU v7x, 32 devices: a whole 2x2x4 slice. The times are simulated.
32 devices in a mesh: groups: 1, ctx: 8 (over z, y), bal: 4 (over x, core), head: 1.
Axes of the slice: x: 2, y: 2, z: 4, core: 2. Of those that a mesh axis runs over, the one named last changes fastest.
Arguments:
- queries: bfloat16 [16384, 2560], P(('groups', 'ctx', 'bal'), 'head'), may hold values from -32 to 32
- keys: bfloat16 [16384, 2560], P(('groups', 'ctx', 'bal'), 'head'), may hold values from -32 to 32
- values: bfloat16 [16384, 2560], P(('groups', 'ctx', 'bal'), 'head'), may hold values from -6 to 6
- output_gradient: bfloat16 [16384, 2560], P(('groups', 'ctx', 'bal'), 'head'), may hold values from -6 to 6
- dilation_phase: int32 [20], P('head'), may hold values from 0 to 127
- segment_device_count: int32 [20], P('head'), may hold values from 1 to 32, as said below
- owner: int32 [128], P('groups'), may hold values from 0 to 127, as said below
Outputs:
- attended: bfloat16 [16384, 2560], P(('groups', 'ctx', 'bal'), 'head')
- query_grad: bfloat16 [16384, 2560], P(('groups', 'ctx', 'bal'), 'head')
- key_grad: bfloat16 [16384, 2560], P(('groups', 'ctx', 'bal'), 'head')
- value_grad: bfloat16 [16384, 2560], P(('groups', 'ctx', 'bal'), 'head')
Inputs may be any that keep to these rules, and one draw needn't show every extreme that they name: `segment_device_count`: every entry is a power of two. The device at index d of the 32 devices of a document (context shard major) holds blocks d * 4 onward. owner is one to one and keeps every block in its context shard of 4 devices: a block of the device at index b of a shard goes to some device e of that shard, into its slot b + t with 0 <= t < 1, and every device hands exactly 1 of its blocks to each device of its shard, itself included.
All inputs are finite; a program needn't handle non-finite values.
Results may differ from a plain program's by a relative error of at most 0.013.
The roundings to bfloat16 on the way count: a program that leaves them out, or rounds other values in their place, can miss the bound.
Values may be sent and summed in bfloat16 or wider, within the bound.
No kernel may reach another device: no remote copies, remote signals or barrier semaphores. Data moves between devices by JAX's collectives and lax.ppermute only.
A program may use at most 128 MiB of HBM per device.

v0:
```python
import functools
import math

import jax
import jax.numpy as jnp
from jax import lax
from jax.experimental import pallas as pl
from jax.experimental.pallas import tpu as pltpu
from jax.sharding import PartitionSpec as P

BLOCK = 128
HEAD = 128
LOG2E = 1.4426950408889634
NT = (((1,), (1,)), ((), ()))
TN = (((0,), (0,)), ((), ()))


def tables(positions, total):
    half = HEAD // 2
    pair = jnp.arange(half, dtype=jnp.float32)
    inverse = jnp.exp(pair * (-2.0 * math.log(10000.0) / HEAD))
    where = positions.astype(jnp.float32)[..., None]
    angles = where * inverse
    base = (2.0 * pair / HEAD + 0.4) / 1.4
    growth = jnp.exp((2.0 * where - total) / total * jnp.log(base))
    cosine, sine = jnp.cos(angles), jnp.sin(angles)

    def pack(scale):
        first, second = cosine * scale, sine * scale
        return (
            jnp.concatenate([first, first], axis=-1),
            jnp.concatenate([-second, second], axis=-1),
        )

    return pack(growth) + pack(1.0 / growth)


def flat_tables(positions, total):
    half = HEAD // 2
    lane = jnp.arange(positions.shape[1] * HEAD, dtype=jnp.int32) % HEAD
    pair = (lane % half).astype(jnp.float32)
    inverse = jnp.exp(pair * (-2.0 * math.log(10000.0) / HEAD))
    where = jnp.repeat(positions.astype(jnp.float32), HEAD, axis=1)
    angles = where * inverse[None, :]
    base = (2.0 * pair / HEAD + 0.4) / 1.4
    growth = jnp.exp((2.0 * where - total) / total * jnp.log(base)[None, :])
    sine = jnp.where(lane[None, :] < half, -jnp.sin(angles), jnp.sin(angles))
    return jnp.cos(angles) / growth, sine / growth


def dot(left, right, dims=None):
    if dims is None:
        dims = (((1,), (0,)), ((), ()))
    return lax.dot_general(left, right, dims, preferred_element_type=jnp.float32)


def attend_kernel(
    per_step, blocks, count, first, relaid, info, phase, seg, far_ref, other_ref, pull_ref, push_ref, *rest
):
    cq_ref, sq_ref, ck_ref, sk_ref = rest[:4]
    own = rest[4:8]
    rest = rest[8:]
    if relaid:
        come, rest = rest[: blocks - 1], rest[blocks - 1 + relaid :]
        finals, rest = rest[:4], rest[4:]
    else:
        finals, rest = rest[:blocks], rest[blocks:]
    pay_ref, near_k, near_v, far_sum = rest
    scale = 1.0 / math.sqrt(HEAD)
    key_at = lax.broadcasted_iota(jnp.int32, (BLOCK, BLOCK), 0)
    query_at = lax.broadcasted_iota(jnp.int32, (BLOCK, BLOCK), 1)
    causal = key_at <= query_at
    far_at = lax.broadcasted_iota(jnp.int32, (count, BLOCK), 0)
    half = HEAD // 2
    for sub in range(per_step):
        head = first + pl.program_id(0) * per_step + sub
        lanes = slice(sub * HEAD, (sub + 1) * HEAD)
        held = jnp.concatenate([far_ref[:, lanes], other_ref[:, lanes]], axis=0)
        both = dot(pull_ref[...], held).astype(jnp.bfloat16)
        far_k, far_v = both[:count], both[count:]
        span = seg[head] * blocks
        p_far, d_far, q_all, g_all = [], [], [], []
        for k in range(blocks):
            if relaid:
                rows = slice(k * BLOCK, (k + 1) * BLOCK)
                source = [ref[:, lanes] for ref in own]
                if k:
                    source = [come[k - 1][t, :, lanes] for t in range(4)]
            else:
                rows = pl.ds(pl.multiple_of(info[k] * BLOCK, BLOCK), BLOCK)
                source = [ref[rows, lanes] for ref in own]
            block = info[blocks + k]
            low = block & (-span)
            cq, sq, ck, sk = cq_ref[rows, :], sq_ref[rows, :], ck_ref[rows, :], sk_ref[rows, :]
            raw_q, raw_k, value, grad = source
            raw_q = raw_q.astype(jnp.float32)
            raw_k = raw_k.astype(jnp.float32)
            tq = (raw_q * cq + pltpu.roll(raw_q, half, 1) * sq).astype(jnp.bfloat16)
            tk = (raw_k * ck + pltpu.roll(raw_k, half, 1) * sk).astype(jnp.bfloat16)
            keys = jnp.concatenate([tk, far_k], axis=0)
            vals = jnp.concatenate([value, far_v], axis=0)
            score = dot(keys, tq, NT)
            allowed = (far_at >= low) & (far_at < block)
            score = jnp.concatenate(
                [
                    jnp.where(causal, score[:BLOCK], -jnp.inf),
                    jnp.where(allowed, score[BLOCK:], -jnp.inf),
                ],
                axis=0,
            )
            top = jnp.max(score, axis=0, keepdims=True)
            weight = jnp.exp2((score - top) * (scale * LOG2E))
            prob = weight * (1.0 / jnp.sum(weight, axis=0, keepdims=True))
            p16 = prob.astype(jnp.bfloat16)
            dprob = dot(vals, grad, NT)
            delta = jnp.sum(p16.astype(jnp.float32) * dprob, axis=0, keepdims=True)
            d16 = (prob * (dprob - delta)).astype(jnp.bfloat16)
            out = dot(p16, vals, TN)
            dq = dot(d16, keys, TN) * scale
            dk = dot(d16[:BLOCK], tq) * scale
            dv = dot(p16[:BLOCK], grad)
            near_k[k] = dk
            near_v[k] = dv
            made = (
                out,
                dq * cq - pltpu.roll(dq, half, 1) * sq,
                dk * ck - pltpu.roll(dk, half, 1) * sk,
                dv,
            )
            for t in range(4):
                if relaid:
                    finals[t][info[2 * blocks + k], :, lanes] = made[t].astype(jnp.bfloat16)
                else:
                    finals[k][t, :, lanes] = made[t].astype(jnp.bfloat16)
            p_far.append(p16[BLOCK:])
            d_far.append(d16[BLOCK:])
            q_all.append(tq)
            g_all.append(grad)
        far_sum[:count] = (
            dot(jnp.concatenate(d_far, axis=1), jnp.concatenate(q_all, axis=0)) * scale
        )
        far_sum[count:] = dot(jnp.concatenate(p_far, axis=1), jnp.concatenate(g_all, axis=0))
        at = phase[head]
        for k in range(blocks):
            block = info[blocks + k]
            far_sum[pl.ds(block, 1), :] = far_sum[pl.ds(block, 1), :] + near_k[k, pl.ds(at, 1), :]
            far_sum[pl.ds(count + block, 1), :] = (
                far_sum[pl.ds(count + block, 1), :] + near_v[k, pl.ds(at, 1), :]
            )
        pay_ref[:, lanes] = dot(push_ref[...], far_sum[...].astype(jnp.bfloat16)).astype(
            jnp.bfloat16
        )


def pick_kernel(
    heads, blocks, phase, k_hbm, v_hbm, cos_ref, sin_ref, after, out_ref, k_ref, v_ref, row_ref,
    load, save
):
    moves = [
        pltpu.make_async_copy(k_hbm, k_ref, load.at[0]),
        pltpu.make_async_copy(v_hbm, v_ref, load.at[1]),
    ]
    for move in moves:
        move.start()
    for move in moves:
        move.wait()
    spot = lax.broadcasted_iota(jnp.int32, (16, HEAD), 0)
    for head in range(heads):
        at = phase[head]
        start = pl.multiple_of(at // 16 * 16, 16)
        lanes = slice(head * HEAD, (head + 1) * HEAD)
        both = []
        for ref in (k_ref, v_ref):
            rows = []
            for k in range(blocks):
                tile = ref[pl.ds(pl.multiple_of(k * BLOCK + start, 16), 16), lanes]
                tile = jnp.where(spot == at - start, tile.astype(jnp.float32), 0.0)
                rows.append(jnp.sum(tile, axis=0, keepdims=True))
            both.append(jnp.concatenate(rows, axis=0))
        key, value = both
        key = key * cos_ref[:, lanes] + pltpu.roll(key, HEAD // 2, 1) * sin_ref[:, lanes]
        row_ref[:, lanes] = jnp.concatenate([key, value], axis=0).astype(jnp.bfloat16)
    copies = [
        pltpu.make_async_copy(row_ref, out_ref.at[d], save.at[d]) for d in range(out_ref.shape[0])
    ]
    for copy in copies:
        copy.start()
    for copy in copies:
        copy.wait()


def pack_kernel(jobs, info, after, *rest):
    number = len(jobs)
    inputs, rest = rest[:4], rest[4:]
    outs, rooms, (load, save) = rest[:number], rest[number : 2 * number], rest[2 * number :]
    order = [(job, t) for job in range(number) for t in range(4)]

    def fetch(job, t):
        k, start, width = jobs[job]
        rows = pl.ds(pl.multiple_of(info[k] * BLOCK, BLOCK), BLOCK)
        source = inputs[t].at[rows, pl.ds(start, width)]
        return pltpu.make_async_copy(source, rooms[job].at[t], load.at[job, t])

    def store(job, t):
        return pltpu.make_async_copy(rooms[job].at[t], outs[job].at[t], save.at[job, t])

    for job, t in order:
        fetch(job, t).start()
    for job, t in order:
        fetch(job, t).wait()
        store(job, t).start()
    for job, t in order:
        store(job, t).wait()


def link_kernel(*refs):
    pass


def place_kernel(number, edge, slot, *rest):
    parts = rest[:number]
    finals = rest[number + 4 : number + 8]
    room, load, save = rest[number + 8 :]
    width = room.shape[-1]

    def save_of(k, t):
        start = pl.multiple_of(slot[k] * BLOCK, BLOCK)
        where = finals[t].at[pl.ds(start, BLOCK), pl.ds(edge, width)]
        return pltpu.make_async_copy(room.at[k, t], where, save.at[k, t])

    loads = [pltpu.make_async_copy(parts[k], room.at[k], load.at[k]) for k in range(number)]
    for move in loads:
        move.start()
    for k in range(number):
        loads[k].wait()
        for t in range(4):
            save_of(k, t).start()
    for k in range(number):
        for t in range(4):
            save_of(k, t).wait()


def patch_kernel(
    heads, blocks, edge, phase, slot, got_hbm, cos_ref, sin_ref, part, *rest
):
    outs = rest[4:8]
    got, room, side, get, load, save, side_load, side_save = rest[8:]
    width = room.shape[-1]
    final = blocks - 1

    def rows(k):
        return pl.ds(pl.multiple_of(slot[k] * BLOCK, BLOCK), BLOCK)

    def left(ref, k):
        return ref.at[:, pl.ds(0, edge if k == final else width)]

    def store(t, k):
        return pltpu.make_async_copy(room.at[t, k], outs[2 + t].at[rows(k)], save.at[t, k])

    order = [(k, t) for k in range(blocks) for t in range(2)]
    fetch = pltpu.make_async_copy(got_hbm, got, get)
    loads = [
        pltpu.make_async_copy(
            left(outs[2 + t].at[rows(k)], k), left(room.at[t, k], k), load.at[t, k]
        )
        for k, t in order
    ]
    right = pl.ds(edge, width - edge)
    side_loads = [pltpu.make_async_copy(part.at[t], side.at[t], side_load.at[t]) for t in range(2)]
    side_loads += [
        pltpu.make_async_copy(part.at[2 + t], room.at[t, final].at[:, right], side_load.at[2 + t])
        for t in range(2)
    ]
    side_saves = [
        pltpu.make_async_copy(side.at[t], outs[t].at[rows(final), right], side_save.at[t])
        for t in range(2)
    ]
    fetch.start()
    for move in loads + side_loads:
        move.start()
    fetch.wait()
    total = got[0].astype(jnp.float32)
    for sender in range(1, got.shape[0]):
        total = total + got[sender].astype(jnp.float32)
    got_sum = total
    spot = lax.broadcasted_iota(jnp.int32, (16, HEAD), 0)
    line = lax.broadcasted_iota(jnp.int32, (2 * blocks, HEAD), 0)
    turned = []
    for head in range(heads):
        lanes = slice(head * HEAD, (head + 1) * HEAD)
        far_k = got_sum[:blocks, lanes]
        turned.append(
            far_k * cos_ref[:, lanes] - pltpu.roll(far_k, HEAD // 2, 1) * sin_ref[:, lanes]
        )
    for t in range(2):
        side_loads[t].wait()
        side_saves[t].start()
    for index, (k, t) in enumerate(order):
        loads[index].wait()
        if k == final:
            side_loads[2 + t].wait()
        for head in range(heads):
            at = phase[head]
            start = pl.multiple_of(at // 16 * 16, 16)
            lanes = slice(head * HEAD, (head + 1) * HEAD)
            old = room[t, k, pl.ds(start, 16), lanes].astype(jnp.float32)
            source = turned[head] if t == 0 else got_sum[blocks:, lanes]
            row = jnp.sum(
                jnp.where(line[:blocks] == slot[k], source, 0.0), axis=0, keepdims=True
            )
            room[t, k, pl.ds(start, 16), lanes] = jnp.where(spot == at - start, row, old).astype(
                jnp.bfloat16
            )
        store(t, k).start()
    for k, t in order:
        store(t, k).wait()
    for move in side_saves:
        move.wait()


def local(queries, keys, values, output_gradient, dilation_phase, segment_device_count, owner):
    rows, width = queries.shape
    heads = width // HEAD
    blocks = rows // BLOCK
    bal_size = lax.axis_size("bal")
    devices = lax.axis_size("ctx") * bal_size
    total = rows * devices
    count = owner.shape[0]
    assert blocks == bal_size == 4 and bal_size & (bal_size - 1) == 0
    bal = lax.axis_index("bal")
    device = lax.axis_index("ctx") * bal_size + bal
    big = pltpu.CompilerParams(vmem_limit_bytes=60 * 1024 * 1024)
    smem = pl.BlockSpec(memory_space=pltpu.SMEM)
    vmem = pl.BlockSpec(memory_space=pltpu.VMEM)
    anywhere = pl.BlockSpec(memory_space=pl.ANY)
    light = pl.CostEstimate(flops=2_000_000_000, bytes_accessed=5_000_000, transcendentals=0)
    heavy = pl.CostEstimate(flops=20_000_000_000, bytes_accessed=60_000_000, transcendentals=0)

    def tokens_of(ids):
        return (ids[:, None] * BLOCK + jnp.arange(BLOCK, dtype=jnp.int32)[None, :]).reshape(rows)

    def swap(array, k):
        return lax.ppermute(array, "bal", [(i, i ^ k) for i in range(bal_size)])

    steps = jnp.arange(blocks, dtype=jnp.int32)
    held = device * blocks + steps
    goes_to = lax.dynamic_slice_in_dim(owner, device * blocks, blocks) // blocks % bal_size
    partner = steps ^ bal
    which = jnp.sum(jnp.where(goes_to[None, :] == partner[:, None], steps[None, :], 0), axis=1)
    info = jnp.concatenate([which, device * blocks + which]).astype(jnp.int32)
    comes_from = jnp.sum(
        jnp.where(
            owner[None, :] == held[:, None], jnp.arange(count, dtype=jnp.int32)[None, :], 0
        ),
        axis=1,
    )

    first = heads // 4 * 2
    last = heads - first
    edge = first * HEAD
    originals = (queries, keys, values, output_gradient)

    def send_inputs(jobs, after):
        sizes = [(4, BLOCK, width) for _, _, width in jobs]
        sent = pl.pallas_call(
            functools.partial(pack_kernel, jobs),
            in_specs=[smem] + [anywhere] * 5,
            out_specs=[anywhere] * len(jobs),
            out_shape=[jax.ShapeDtypeStruct(size, jnp.bfloat16) for size in sizes],
            scratch_shapes=[pltpu.VMEM(size, jnp.bfloat16) for size in sizes]
            + [pltpu.SemaphoreType.DMA((len(jobs), 4))] * 2,
            compiler_params=big,
        )(info, after, *originals)
        return sent, [swap(one, job[0]) for one, job in zip(sent, jobs)]

    sent, come_early = send_inputs([(2, 0, edge)], owner)

    cq, sq, ck, sk = tables(tokens_of(held), total)
    own_phase = (held[:, None] * BLOCK + dilation_phase[None, :]).astype(jnp.int32)
    pick_cos, pick_sin = flat_tables(own_phase, total)
    own_far = pl.pallas_call(
        functools.partial(pick_kernel, heads, blocks),
        in_specs=[smem, anywhere, anywhere, vmem, vmem, anywhere],
        out_specs=anywhere,
        out_shape=jax.ShapeDtypeStruct((devices // 2, 2 * blocks, width), jnp.bfloat16),
        scratch_shapes=[
            pltpu.VMEM((rows, width), jnp.bfloat16),
            pltpu.VMEM((rows, width), jnp.bfloat16),
            pltpu.VMEM((2 * blocks, width), jnp.bfloat16),
            pltpu.SemaphoreType.DMA((2,)),
            pltpu.SemaphoreType.DMA((devices // 2,)),
        ],
        compiler_params=big,
    )(
        dilation_phase,
        keys,
        values,
        pick_cos,
        pick_sin,
        sent[0],
    )
    halves = [list(range(0, devices, 2)), list(range(1, devices, 2))]
    near_far = lax.all_to_all(
        own_far,
        ("ctx", "bal"),
        split_axis=0,
        concat_axis=0,
        tiled=True,
        axis_index_groups=halves,
    ).reshape(count, width)
    other_far = swap(near_far, 1)
    later = [3, 1]
    _, come_late = send_inputs([(k, 0, edge) for k in later], own_far)
    come = dict(zip([2] + later, come_early + come_late))
    come = [come[k] for k in range(1, blocks)]

    side = 2 * count
    wide = jnp.arange(side, dtype=jnp.int32)
    tall = wide[:, None]
    wide = wide[None, :]
    source = tall % count
    holder = source // blocks
    held_row = (holder ^ device) % 2 * count + holder // 2 * (2 * blocks)
    pull = (wide == held_row + tall // count * blocks + source % blocks).astype(jnp.bfloat16)
    lands = owner // blocks * (2 * blocks) + owner % blocks
    push = (jnp.concatenate([lands, lands + blocks])[None, :] == tall).astype(jnp.bfloat16)

    per_step = 2
    columns = per_step * HEAD
    fixed = lambda h, *_: (0, 0)
    square = pl.BlockSpec((side, side), fixed)
    table = pl.BlockSpec((rows, HEAD), fixed)
    part = pl.BlockSpec((4, BLOCK, columns), lambda h, *_: (0, 0, h))
    scratch = [
        pltpu.VMEM((blocks, BLOCK, HEAD), jnp.float32),
        pltpu.VMEM((blocks, BLOCK, HEAD), jnp.float32),
        pltpu.VMEM((side, HEAD), jnp.float32),
    ]
    skip = first // per_step
    tensor = pl.BlockSpec((rows, columns), lambda h, *_: (0, h + skip))
    lane = pl.BlockSpec((side, columns), lambda h, *_: (0, h + skip))
    far = pl.BlockSpec((count, columns), lambda h, *_: (0, h + skip))
    results = pl.pallas_call(
        functools.partial(attend_kernel, per_step, blocks, count, first, 0),
        grid_spec=pltpu.PrefetchScalarGridSpec(
            num_scalar_prefetch=3,
            grid=(last // per_step,),
            in_specs=[far, far, square, square] + [table] * 4 + [tensor] * 4,
            out_specs=[part] * blocks + [lane],
            scratch_shapes=scratch,
        ),
        out_shape=[jax.ShapeDtypeStruct((4, BLOCK, last * HEAD), jnp.bfloat16)] * blocks
        + [jax.ShapeDtypeStruct((side, width), jnp.bfloat16)],
        compiler_params=big,
        cost_estimate=heavy,
    )(
        info,
        dilation_phase,
        segment_device_count,
        near_far,
        other_far,
        pull,
        push,
        cq,
        sq,
        ck,
        sk,
        *originals,
    )
    parts, payload = list(results[:blocks]), results[blocks]
    for k in range(1, blocks):
        parts[k] = swap(parts[k], k)

    ids = (device ^ steps) * blocks
    came = jnp.sum(
        jnp.where(comes_from[None, :] // blocks * blocks == ids[:, None], comes_from[None, :], 0),
        axis=1,
    )
    moved = jnp.concatenate([which, came, partner]).astype(jnp.int32)
    cq, sq, ck, sk = tables(tokens_of(came), total)
    shapes = [jax.ShapeDtypeStruct((blocks, BLOCK, width), jnp.bfloat16)] * 4
    shapes = shapes + [jax.ShapeDtypeStruct((side, width), jnp.bfloat16)]

    def attend_relaid(begin, end, come, carried):
        skip = begin // per_step
        tensor = pl.BlockSpec((BLOCK, columns), lambda h, info, *_: (info[0], h + skip))
        lane = pl.BlockSpec((side, columns), lambda h, *_: (0, h + skip))
        far = pl.BlockSpec((count, columns), lambda h, *_: (0, h + skip))
        whole = pl.BlockSpec((blocks, BLOCK, columns), lambda h, *_: (0, 0, h + skip))
        operands = 3 + 4 + 4 + 4 + blocks - 1
        return pl.pallas_call(
            functools.partial(attend_kernel, per_step, blocks, count, begin, len(carried)),
            grid_spec=pltpu.PrefetchScalarGridSpec(
                num_scalar_prefetch=3,
                grid=((end - begin) // per_step,),
                in_specs=[far, far, square, square]
                + [table] * 4
                + [tensor] * 4
                + [part] * (blocks - 1)
                + [anywhere] * len(carried),
                out_specs=[whole] * 4 + [lane],
                scratch_shapes=scratch,
            ),
            out_shape=shapes,
            input_output_aliases={
                operands + i: 5 - len(carried) + i for i in range(len(carried))
            },
            compiler_params=big,
            cost_estimate=light,
        )(
            moved,
            dilation_phase,
            segment_device_count,
            near_far,
            other_far,
            pull,
            push,
            cq,
            sq,
            ck,
            sk,
            *originals,
            *come,
            *carried,
        )

    results = attend_relaid(0, first, come, [payload])
    finals, payload = [one.reshape(rows, width) for one in results[:4]], results[4]
    payload = pl.pallas_call(
        link_kernel,
        in_specs=[anywhere, anywhere],
        out_specs=anywhere,
        out_shape=jax.ShapeDtypeStruct((side, width), jnp.bfloat16),
        input_output_aliases={0: 0},
        compiler_params=pltpu.CompilerParams(
            vmem_limit_bytes=60 * 1024 * 1024, has_side_effects=True
        ),
    )(payload, parts[2])
    got = lax.all_to_all(
        payload.reshape(devices, 2 * blocks, width),
        ("ctx", "bal"),
        split_axis=0,
        concat_axis=0,
        tiled=True,
    )

    new_phase = (comes_from[:, None] * BLOCK + dilation_phase[None, :]).astype(jnp.int32)
    new_cos, new_sin = flat_tables(new_phase, total)
    out = jax.ShapeDtypeStruct((rows, width), jnp.bfloat16)
    number = blocks - 1
    slots = partner.astype(jnp.int32)
    finals = pl.pallas_call(
        functools.partial(place_kernel, number, edge),
        in_specs=[smem] + [anywhere] * (number + 4),
        out_specs=[anywhere] * 4,
        out_shape=[out] * 4,
        input_output_aliases={1 + number + t: t for t in range(4)},
        scratch_shapes=[
            pltpu.VMEM((number, 4, BLOCK, last * HEAD), jnp.bfloat16),
            pltpu.SemaphoreType.DMA((number,)),
            pltpu.SemaphoreType.DMA((number, 4)),
        ],
        compiler_params=big,
        cost_estimate=light,
    )(slots, *parts[:number], *finals)
    return tuple(
        pl.pallas_call(
            functools.partial(patch_kernel, heads, blocks, edge),
            in_specs=[smem, smem, anywhere, vmem, vmem] + [anywhere] * 5,
            out_specs=[anywhere] * 4,
            out_shape=[out] * 4,
            input_output_aliases={6 + t: t for t in range(4)},
            scratch_shapes=[
                pltpu.VMEM((devices, 2 * blocks, width), jnp.bfloat16),
                pltpu.VMEM((2, blocks, BLOCK, width), jnp.bfloat16),
                pltpu.VMEM((2, BLOCK, last * HEAD), jnp.bfloat16),
                pltpu.SemaphoreType.DMA(()),
                pltpu.SemaphoreType.DMA((2, blocks)),
                pltpu.SemaphoreType.DMA((2, blocks)),
                pltpu.SemaphoreType.DMA((4,)),
                pltpu.SemaphoreType.DMA((2,)),
            ],
            compiler_params=big,
        )(
            dilation_phase,
            slots,
            got,
            new_cos,
            new_sin,
            parts[number],
            *finals,
        )
    )


def solution(mesh):
    token = P(("groups", "ctx", "bal"), "head")
    return jax.shard_map(
        local,
        mesh=mesh,
        in_specs=(token, token, token, token, P("head"), P("head"), P("groups")),
        out_specs=(token, token, token, token),
        check_vma=False,
    )
```

profile of v0, /device:TPU:0, one launch (start us, length us, event | category | flops | bytes accessed | tf_op | source)
XLA Modules:
  0.0 164.1 jit_solution(8356747865099278739)
XLA Ops:
  0.6 0.7 and_select_fusion.9
  2.1 2.9 %shard_map.102.after = bf16[4,128,1280]{2,1,0:T(8,128)(2,1)} custom-call(s32[8]{0:T(128)} %pad_add_fusion.2.info, s32[128]{0:T(128)} %after.1, bf16[512,2560]{1,0:T(8,128)(2,1)} %rest_4_.3, bf16[512,2560]{1,0:T(8,128)(2,1)} %rest_5_.3, bf16[512,2560]{1,0:T(8,128)(2,1)} %rest_6_.3, bf16[512,2560]{1,0:T(8,128)(2,1)} %rest_7_.3), custom_call_target="tpu_custom_call" | custom-call | tf_op jit(solution)/shard_map/pallas_call | solution.py:365
  5.0 3.0 %collective-permute-start.2 = (bf16[4,128,1280]{2,1,0:T(8,128)(2,1)}, bf16[4,128,1280]{2,1,0:T(8,128)(2,1)}, u32[]{:S(2)}, u32[]{:S(2)}) collective-permute-start(bf16[4,128,1280]{2,1,0:T(8,128)(2,1)} %shard_map.102.after), channel_id=1, source_target_pairs={{0,2},{1,3},{2,0},{3,1},{4,6},{5,7},{6,4},{7,5},{8,10},{9,11},{10,... | collective-permute-start | bytes 3932168 | tf_op jit(solution)/shard_map/ppermute | solution.py:343
  8.5 1.3 fusion.17
  9.8 4.7 %shard_map.103.after = bf16[16,8,2560]{2,1,0:T(8,128)(2,1)} custom-call(s32[20]{0:T(128)} %phase.7, bf16[512,2560]{1,0:T(8,128)(2,1)} %rest_5_.3, bf16[512,2560]{1,0:T(8,128)(2,1)} %rest_6_.3, f32[4,2560]{1,0:T(4,128)} %get-tuple-element.42.cos_ref, f32[4,2560]{1,0:T(4,128)} %get-tuple-element.43.sin_ref, bf16[4,128,1280]{2,1,0:T(8,128)(2,1)} %shard_map.102.after), custom_call_target="tpu_custom_call" | custom-call | tf_op jit(solution)/shard_map/pallas_call | solution.py:381
  14.5 6.0 %all-to-all-start = ((bf16[16,8,2560]{2,1,0:T(8,128)(2,1)}), bf16[16,8,2560]{2,1,0:T(8,128)(2,1)S(1)}, u32[]{:S(2)}, u32[]{:S(2)}) async-start(bf16[16,8,2560]{2,1,0:T(8,128)(2,1)} %shard_map.103.after), calls=%async_computation | async-start | bytes 1310720 | tf_op jit(solution)/shard_map/all_to_all | solution.py:403
  20.4 3.3 %shard_map.104 = (bf16[4,128,1280]{2,1,0:T(8,128)(2,1)}, bf16[4,128,1280]{2,1,0:T(8,128)(2,1)}) custom-call(s32[8]{0:T(128)} %pad_add_fusion.2.info, bf16[16,8,2560]{2,1,0:T(8,128)(2,1)} %shard_map.103.after, bf16[512,2560]{1,0:T(8,128)(2,1)} %rest_4_.3, bf16[512,2560]{1,0:T(8,128)(2,1)} %rest_5_.3, bf16[512,2560]{1,0:T(8,128)(2,1)} %rest_6_.3, ...), custom_call_target="tpu_custom_call" | custom-call | tf_op jit(solution)/shard_map/pallas_call | solution.py:365
  23.8 2.0 %collective-permute-start.3 = (bf16[4,128,1280]{2,1,0:T(8,128)(2,1)}, bf16[4,128,1280]{2,1,0:T(8,128)(2,1)}, u32[]{:S(2)}, u32[]{:S(2)}) collective-permute-start(bf16[4,128,1280]{2,1,0:T(8,128)(2,1)} %get-tuple-element.21), channel_id=1, source_target_pairs={{0,3},{1,2},{2,1},{3,0},{4,7},{5,6},{6,5},{7,4},{8,11},{9,10},{10,... | collective-permute-start | bytes 3932168 | tf_op jit(solution)/shard_map/ppermute | solution.py:343
  26.4 2.8 %fusion.13 = (f32[512,64]{1,0:T(8,128)S(1)}, f32[512,64]{1,0:T(8,128)S(1)}, f32[512,64]{1,0:T(8,128)S(1)}, f32[512,64]{1,0:T(8,128)S(1)}, f32[512,64]{1,0:T(8,12...) fusion(f32[64]{0:T(128)S(1)} %get-tuple-element.72, ...), kind=kLoop, calls=%fused_computation.31 | loop fusion | flops 589824 | bytes 1581568 | tf_op jit(solution)/shard_map/neg | solution.py:32
  29.2 0.8 pad_maximum_fusion.4.rest_0_
  30.0 15.5 %all-to-all-done = bf16[16,8,2560]{2,1,0:T(8,128)(2,1)S(1)} async-done(((bf16[16,8,2560]{2,1,0:T(8,128)(2,1)}), bf16[16,8,2560]{2,1,0:T(8,128)(2,1)S(1)}, u32[]{:S(2)}, u32[]{:S(2)}) %all-to-all-start) | async-done | bytes 655392 | tf_op jit(solution)/shard_map/all_to_all | solution.py:403
  45.5 1.0 pad_maximum_fusion.6.rest_2_
  46.5 0.9 pad_maximum_fusion.7.rest_3_
  47.3 0.8 pad_maximum_fusion.5.rest_1_
  48.2 0.8 fusion.10
  49.0 0.8 copy-done.5
  49.8 23.3 %shard_map.105 = (bf16[4,128,1280]{2,1,0:T(8,128)(2,1)}, bf16[4,128,1280]{2,1,0:T(8,128)(2,1)}, bf16[4,128,1280]{2,1,0:T(8,128)(2,1)}, bf16[4,128,1280]{2,1,0:T(8,128)(2,1)}, bf16[256,2560]{1,0:T(8,128)(2,1)}) custom-call(s32[8]{0:T(128)} %pad_add_fusion.2.info, s32[20]{0:T(128)} %phase.7, s32[20]{0:T(128)} %seg.3, bf16[128,2560]{1,0:T(8,128)(2,1)} %bitcast.58, ...), custom_call_target="tpu_custom_call" | custom-call | flops 20000000000 | bytes 60000000 | tf_op jit(solution)/shard_map/pallas_call | solution.py:443
  73.1 2.4 %collective-permute-start.4 = (bf16[4,128,1280]{2,1,0:T(8,128)(2,1)}, bf16[4,128,1280]{2,1,0:T(8,128)(2,1)S(1)}, u32[]{:S(2)}, u32[]{:S(2)}) collective-permute-start(bf16[4,128,1280]{2,1,0:T(8,128)(2,1)} %get-tuple-element.24), channel_id=1, source_target_pairs={{0,2},{1,3},{2,0},{3,1},{4,6},{5,7},{6,4},{7,5},{8,10},{9,11},{10,... | collective-permute-start | bytes 3932168 | tf_op jit(solution)/shard_map/ppermute | solution.py:343
  76.1 0.8 pad_maximum_fusion.rest_0_
  76.9 0.8 pad_maximum_fusion.2.rest_2_
  77.8 0.9 pad_maximum_fusion.3.rest_3_
  78.6 0.8 pad_maximum_fusion.1.rest_1_
  79.5 22.8 %shard_map.106 = (bf16[4,128,2560]{2,1,0:T(8,128)(2,1)}, bf16[4,128,2560]{2,1,0:T(8,128)(2,1)}, bf16[4,128,2560]{2,1,0:T(8,128)(2,1)}, bf16[4,128,2560]{2,1,0:T(8,128)(2,1)}, bf16[256,2560]{1,0:T(8,128)(2,1)}) custom-call(s32[12]{0:T(128)} %pad_add_fusion.1.info, s32[20]{0:T(128)} %phase.7, s32[20]{0:T(128)} %seg.3, ...), custom_call_target="tpu_custom_call", output_to_operand_aliasing={{4}: (18, {})} | custom-call | flops 2000000000 | bytes 5000000 | tf_op jit(solution)/shard_map/pallas_call | solution.py:491
  102.3 2.8 %collective-permute-done.4.refs_1_.rest_2_ = bf16[4,128,1280]{2,1,0:T(8,128)(2,1)S(1)} collective-permute-done((bf16[4,128,1280]{2,1,0:T(8,128)(2,1)}, bf16[4,128,1280]{2,1,0:T(8,128)(2,1)S(1)}, u32[]{:S(2)}, u32[]{:S(2)}) %collective-permute-start.4) | collective-permute-done | bytes 1310752 | tf_op jit(solution)/shard_map/ppermute | solution.py:343
  105.0 1.1 copy-done.1
  106.1 5.2 %all-to-all-start.1 = ((bf16[32,8,2560]{2,1,0:T(8,128)(2,1)}), bf16[32,8,2560]{2,1,0:T(8,128)(2,1)S(1)}, u32[]{:S(2)}, u32[]{:S(2)}) async-start(bf16[32,8,2560]{2,1,0:T(8,128)(2,1)} %bitcast.52), calls=%async_computation.1 | async-start | bytes 2621440 | tf_op jit(solution)/shard_map/all_to_all | solution.py:539
  111.6 1.6 collective-permute-start.5
  113.3 1.5 collective-permute-done.6.rest_1_
  114.8 4.0 %shard_map.108 = (bf16[512,2560]{1,0:T(8,128)(2,1)}, bf16[512,2560]{1,0:T(8,128)(2,1)}, bf16[512,2560]{1,0:T(8,128)(2,1)}, bf16[512,2560]{1,0:T(8,128)(2,1)}) custom-call(s32[4]{0:T(128)} %copy-done.6, bf16[4,128,1280]{2,1,0:T(8,128)(2,1)} %get-tuple-element.26.rest_0_, ...), custom_call_target="tpu_custom_call", output_to_operand_aliasing={{0}: (4, {}), {1}: (5, {}), {2}: (6, {}), {3}: (7, {})} | custom-call | flops 2000000000 | bytes 5000000 | tf_op jit(solution)/shard_map/pallas_call | solution.py:552
  118.8 37.0 %collective-permute-done.5.part = bf16[4,128,1280]{2,1,0:T(8,128)(2,1)S(1)} collective-permute-done((bf16[4,128,1280]{2,1,0:T(8,128)(2,1)}, bf16[4,128,1280]{2,1,0:T(8,128)(2,1)S(1)}, u32[]{:S(2)}, u32[]{:S(2)}) %collective-permute-start.5) | collective-permute-done | bytes 1310752 | tf_op jit(solution)/shard_map/ppermute | solution.py:343
  155.8 1.1 copy-done.3
  157.3 6.8 %shard_map.109 = (bf16[512,2560]{1,0:T(8,128)(2,1)}, bf16[512,2560]{1,0:T(8,128)(2,1)}, bf16[512,2560]{1,0:T(8,128)(2,1)}, bf16[512,2560]{1,0:T(8,128)(2,1)}) custom-call(s32[20]{0:T(128)} %phase.7, s32[4]{0:T(128)} %copy-done.6, bf16[32,8,2560]{2,1,0:T(8,128)(2,1)} %copy-done, ...), custom_call_target="tpu_custom_call", output_to_operand_aliasing={{0}: (6, {}), {1}: (7, {}), {2}: (8, {}), {3}: (9, {})} | custom-call | tf_op jit(solution)/shard_map/pallas_call | solution.py:567
  (47 shorter events, 3.2 us)
Async XLA Ops:
  1.4 74.2 %copy-start.6 = (s32[4]{0:T(128)}, s32[4]{0:T(128)S(1)}, u32[]{:S(2)}) copy-start(s32[4]{0:T(128)S(1)} %get-tuple-element.69.slot) | copy-start | bytes 52
  2.1 5.9 %copy-start.8 = (s32[128]{0:T(128)S(1)}, s32[128]{0:T(128)}, u32[]{:S(2)}) copy-start(s32[128]{0:T(128)} %after.1) | copy-start | bytes 1540
  2.1 6.1 %copy-start.7 = (s32[20]{0:T(128)S(1)}, s32[20]{0:T(128)}, u32[]{:S(2)}) copy-start(s32[20]{0:T(128)} %phase.7) | copy-start | bytes 244
  5.0 74.4 %collective-permute-start.2 = (bf16[4,128,1280]{2,1,0:T(8,128)(2,1)}, bf16[4,128,1280]{2,1,0:T(8,128)(2,1)}, u32[]{:S(2)}, u32[]{:S(2)}) collective-permute-start(bf16[4,128,1280]{2,1,0:T(8,128)(2,1)} %shard_map.102.after), channel_id=1, source_target_pairs={{0,2},{1,3},{2,0},{3,1},{4,6},{5,7},{6,4},{7,5},{8,10},{9,11},{10,... | collective-permute-start | bytes 3932168 | tf_op jit(solution)/shard_map/ppermute | solution.py:343
  14.5 31.0 %all-to-all-start = ((bf16[16,8,2560]{2,1,0:T(8,128)(2,1)}), bf16[16,8,2560]{2,1,0:T(8,128)(2,1)S(1)}, u32[]{:S(2)}, u32[]{:S(2)}) async-start(bf16[16,8,2560]{2,1,0:T(8,128)(2,1)} %shard_map.103.after), calls=%async_computation | async-start | bytes 1310720 | tf_op jit(solution)/shard_map/all_to_all | solution.py:403
  23.7 55.8 %collective-permute-start.1 = (bf16[4,128,1280]{2,1,0:T(8,128)(2,1)}, bf16[4,128,1280]{2,1,0:T(8,128)(2,1)}, u32[]{:S(2)}, u32[]{:S(2)}) collective-permute-start(bf16[4,128,1280]{2,1,0:T(8,128)(2,1)} %get-tuple-element.20), channel_id=1, source_target_pairs={{0,1},{1,0},{2,3},{3,2},{4,5},{5,4},{6,7},{7,6},{8,9},{9,8},{10,11... | collective-permute-start | bytes 3932168 | tf_op jit(solution)/shard_map/ppermute | solution.py:343
  23.8 55.7 %collective-permute-start.3 = (bf16[4,128,1280]{2,1,0:T(8,128)(2,1)}, bf16[4,128,1280]{2,1,0:T(8,128)(2,1)}, u32[]{:S(2)}, u32[]{:S(2)}) collective-permute-start(bf16[4,128,1280]{2,1,0:T(8,128)(2,1)} %get-tuple-element.21), channel_id=1, source_target_pairs={{0,3},{1,2},{2,1},{3,0},{4,7},{5,6},{6,5},{7,4},{8,11},{9,10},{10,... | collective-permute-start | bytes 3932168 | tf_op jit(solution)/shard_map/ppermute | solution.py:343
  45.5 4.3 %copy-start.2 = (bf16[16,8,2560]{2,1,0:T(8,128)(2,1)}, bf16[16,8,2560]{2,1,0:T(8,128)(2,1)S(1)}, u32[]{:S(2)}) copy-start(bf16[16,8,2560]{2,1,0:T(8,128)(2,1)S(1)} %all-to-all-done) | copy-start | bytes 1966084
  45.5 3.4 %collective-permute-start = (bf16[128,2560]{1,0:T(8,128)(2,1)S(1)}, bf16[128,2560]{1,0:T(8,128)(2,1)S(1)}, u32[]{:S(2)}, u32[]{:S(2)}) collective-permute-start(bf16[128,2560]{1,0:T(8,128)(2,1)S(1)} %bitcast.57), channel_id=1, source_target_pairs={{0,1},{1,0},{2,3},{3,2},{4,5},{5,4},{6,7},{7,6},{8,9},{9,8},{10,11... | collective-permute-start | bytes 1966088 | tf_op jit(solution)/shard_map/ppermute | solution.py:343
  49.0 0.8 copy-start.5
  49.8 26.3 %copy-start.4 = (f32[512,64]{1,0:T(8,128)S(1)}, f32[512,64]{1,0:T(8,128)}, u32[]{:S(2)}) copy-start(f32[512,64]{1,0:T(8,128)} %get-tuple-element.56) | copy-start | bytes 393220
  73.1 31.9 %collective-permute-start.4 = (bf16[4,128,1280]{2,1,0:T(8,128)(2,1)}, bf16[4,128,1280]{2,1,0:T(8,128)(2,1)S(1)}, u32[]{:S(2)}, u32[]{:S(2)}) collective-permute-start(bf16[4,128,1280]{2,1,0:T(8,128)(2,1)} %get-tuple-element.24), channel_id=1, source_target_pairs={{0,2},{1,3},{2,0},{3,1},{4,6},{5,7},{6,4},{7,5},{8,10},{9,11},{10,... | collective-permute-start | bytes 3932168 | tf_op jit(solution)/shard_map/ppermute | solution.py:343
  105.0 1.1 copy-start.1
  106.1 49.7 %all-to-all-start.1 = ((bf16[32,8,2560]{2,1,0:T(8,128)(2,1)}), bf16[32,8,2560]{2,1,0:T(8,128)(2,1)S(1)}, u32[]{:S(2)}, u32[]{:S(2)}) async-start(bf16[32,8,2560]{2,1,0:T(8,128)(2,1)} %bitcast.52), calls=%async_computation.1 | async-start | bytes 2621440 | tf_op jit(solution)/shard_map/all_to_all | solution.py:539
  111.3 3.4 %collective-permute-start.6 = (bf16[4,128,1280]{2,1,0:T(8,128)(2,1)}, bf16[4,128,1280]{2,1,0:T(8,128)(2,1)}, u32[]{:S(2)}, u32[]{:S(2)}) collective-permute-start(bf16[4,128,1280]{2,1,0:T(8,128)(2,1)} %get-tuple-element.27), channel_id=1, source_target_pairs={{0,1},{1,0},{2,3},{3,2},{4,5},{5,4},{6,7},{7,6},{8,9},{9,8},{10,11... | collective-permute-start | bytes 3932168 | tf_op jit(solution)/shard_map/ppermute | solution.py:343
  111.6 44.2 %collective-permute-start.5 = (bf16[4,128,1280]{2,1,0:T(8,128)(2,1)}, bf16[4,128,1280]{2,1,0:T(8,128)(2,1)S(1)}, u32[]{:S(2)}, u32[]{:S(2)}) collective-permute-start(bf16[4,128,1280]{2,1,0:T(8,128)(2,1)} %get-tuple-element.25), channel_id=1, source_target_pairs={{0,3},{1,2},{2,1},{3,0},{4,7},{5,6},{6,5},{7,4},{8,11},{9,10},{10,... | collective-permute-start | bytes 3932168 | tf_op jit(solution)/shard_map/ppermute | solution.py:343
  155.8 1.1 copy-start.3
  155.8 1.5 copy-start
where the time goes:
time: 165 us; the launch traced here: 164 us
  Pallas kernels  67.8 us (41%)
  waiting for transfers between devices  56.8 us (34%)
  starting transfers between devices  20.6 us (12%)
  other arithmetic  14.6 us (9%)
  local copies, waits for them, and re-layouts  3.58 us (2%)
    ppermute x7, waiting for transfers between devices, swap(): return lax.ppermute(array, 'bal', [(i, i ^ k) for i in range(bal_size)])  41.3 us
    pallas_call x1, Pallas kernels, local(): pl.pallas_call(functools.partial(attend_kernel, per_step, blocks, count,...  23.3 us
    pallas_call x1, Pallas kernels, attend_relaid(): pl.pallas_call(functools.partial(attend_kernel, per_step, blocks, count,...  22.8 us
    all_to_all x1, waiting for transfers between devices, local(): lax.all_to_all(own_far, ('ctx', 'bal'), split_axis=0, concat_axis=0, tile...  15.5 us
    ppermute x7, starting transfers between devices, swap(): return lax.ppermute(array, 'bal', [(i, i ^ k) for i in range(bal_size)])  9.49 us
    pallas_call x1, Pallas kernels, local(): pl.pallas_call(functools.partial(patch_kernel, heads, blocks, edge), in_s...  6.82 us
    pallas_call x2, Pallas kernels, send_inputs(): pl.pallas_call(functools.partial(pack_kernel, jobs), in_specs=[smem] + [a...  6.14 us
    all_to_all x1, starting transfers between devices, local(): lax.all_to_all(own_far, ('ctx', 'bal'), split_axis=0, concat_axis=0, tile...  5.95 us
  transfers between devices with their start and end apart: 9, of which 4 were waited for; matrix products, arithmetic and copies ran while one was open for 8% of the time, Pallas kernels for 35%

commit v1 on v0

--- a/solution.py
+++ b/solution.py
@@ -65,12 +65,12 @@
         finals, rest = rest[:4], rest[4:]
     else:
         finals, rest = rest[:blocks], rest[blocks:]
-    pay_ref, near_k, near_v, far_sum = rest
+    (pay_ref,) = rest
     scale = 1.0 / math.sqrt(HEAD)
     key_at = lax.broadcasted_iota(jnp.int32, (BLOCK, BLOCK), 0)
     query_at = lax.broadcasted_iota(jnp.int32, (BLOCK, BLOCK), 1)
-    causal = key_at <= query_at
     far_at = lax.broadcasted_iota(jnp.int32, (count, BLOCK), 0)
+    far_query = lax.broadcasted_iota(jnp.int32, (count, BLOCK), 1)
     half = HEAD // 2
     for sub in range(per_step):
         head = first + pl.program_id(0) * per_step + sub
@@ -79,6 +79,9 @@
         both = dot(pull_ref[...], held).astype(jnp.bfloat16)
         far_k, far_v = both[:count], both[count:]
         span = seg[head] * blocks
+        at = phase[head]
+        causal = (key_at <= query_at) & (key_at != at)
+        behind = far_at * BLOCK + at - far_query
         p_far, d_far, q_all, g_all = [], [], [], []
         for k in range(blocks):
             if relaid:
@@ -100,7 +103,7 @@
             keys = jnp.concatenate([tk, far_k], axis=0)
             vals = jnp.concatenate([value, far_v], axis=0)
             score = dot(keys, tq, NT)
-            allowed = (far_at >= low) & (far_at < block)
+            allowed = (far_at >= low) & (behind <= block * BLOCK)
             score = jnp.concatenate(
                 [
                     jnp.where(causal, score[:BLOCK], -jnp.inf),
@@ -119,8 +122,6 @@
             dq = dot(d16, keys, TN) * scale
             dk = dot(d16[:BLOCK], tq) * scale
             dv = dot(p16[:BLOCK], grad)
-            near_k[k] = dk
-            near_v[k] = dv
             made = (
                 out,
                 dq * cq - pltpu.roll(dq, half, 1) * sq,
@@ -136,20 +137,10 @@
             d_far.append(d16[BLOCK:])
             q_all.append(tq)
             g_all.append(grad)
-        far_sum[:count] = (
-            dot(jnp.concatenate(d_far, axis=1), jnp.concatenate(q_all, axis=0)) * scale
-        )
-        far_sum[count:] = dot(jnp.concatenate(p_far, axis=1), jnp.concatenate(g_all, axis=0))
-        at = phase[head]
-        for k in range(blocks):
-            block = info[blocks + k]
-            far_sum[pl.ds(block, 1), :] = far_sum[pl.ds(block, 1), :] + near_k[k, pl.ds(at, 1), :]
-            far_sum[pl.ds(count + block, 1), :] = (
-                far_sum[pl.ds(count + block, 1), :] + near_v[k, pl.ds(at, 1), :]
-            )
-        pay_ref[:, lanes] = dot(push_ref[...], far_sum[...].astype(jnp.bfloat16)).astype(
-            jnp.bfloat16
-        )
+        far_dk = dot(jnp.concatenate(d_far, axis=1), jnp.concatenate(q_all, axis=0)) * scale
+        far_dv = dot(jnp.concatenate(p_far, axis=1), jnp.concatenate(g_all, axis=0))
+        far_sum = jnp.concatenate([far_dk, far_dv], axis=0).astype(jnp.bfloat16)
+        pay_ref[:, lanes] = dot(push_ref[...], far_sum).astype(jnp.bfloat16)
 
 
 def pick_kernel(
@@ -329,7 +320,8 @@
     assert blocks == bal_size == 4 and bal_size & (bal_size - 1) == 0
     bal = lax.axis_index("bal")
     device = lax.axis_index("ctx") * bal_size + bal
-    big = pltpu.CompilerParams(vmem_limit_bytes=60 * 1024 * 1024)
+    room = 66_000_000
+    big = pltpu.CompilerParams(vmem_limit_bytes=room)
     smem = pl.BlockSpec(memory_space=pltpu.SMEM)
     vmem = pl.BlockSpec(memory_space=pltpu.VMEM)
     anywhere = pl.BlockSpec(memory_space=pl.ANY)
@@ -355,7 +347,7 @@
         axis=1,
     )
 
-    first = heads // 4 * 2
+    first = heads * 3 // 10 * 2
     last = heads - first
     edge = first * HEAD
     originals = (queries, keys, values, output_gradient)
@@ -431,11 +423,6 @@
     square = pl.BlockSpec((side, side), fixed)
     table = pl.BlockSpec((rows, HEAD), fixed)
     part = pl.BlockSpec((4, BLOCK, columns), lambda h, *_: (0, 0, h))
-    scratch = [
-        pltpu.VMEM((blocks, BLOCK, HEAD), jnp.float32),
-        pltpu.VMEM((blocks, BLOCK, HEAD), jnp.float32),
-        pltpu.VMEM((side, HEAD), jnp.float32),
-    ]
     skip = first // per_step
     tensor = pl.BlockSpec((rows, columns), lambda h, *_: (0, h + skip))
     lane = pl.BlockSpec((side, columns), lambda h, *_: (0, h + skip))
@@ -447,7 +434,6 @@
             grid=(last // per_step,),
             in_specs=[far, far, square, square] + [table] * 4 + [tensor] * 4,
             out_specs=[part] * blocks + [lane],
-            scratch_shapes=scratch,
         ),
         out_shape=[jax.ShapeDtypeStruct((4, BLOCK, last * HEAD), jnp.bfloat16)] * blocks
         + [jax.ShapeDtypeStruct((side, width), jnp.bfloat16)],
@@ -499,8 +485,7 @@
                 + [part] * (blocks - 1)
                 + [anywhere] * len(carried),
                 out_specs=[whole] * 4 + [lane],
-                scratch_shapes=scratch,
-            ),
+                ),
             out_shape=shapes,
             input_output_aliases={
                 operands + i: 5 - len(carried) + i for i in range(len(carried))
@@ -533,7 +518,7 @@
         out_shape=jax.ShapeDtypeStruct((side, width), jnp.bfloat16),
         input_output_aliases={0: 0},
         compiler_params=pltpu.CompilerParams(
-            vmem_limit_bytes=60 * 1024 * 1024, has_side_effects=True
+            vmem_limit_bytes=room, has_side_effects=True
         ),
     )(payload, parts[2])
     got = lax.all_to_all(

time: 165 us -> 163 us (0.988)
  other arithmetic: 14.6 us -> 19.3 us
  waiting for transfers between devices: 56.8 us -> 53.8 us
  local copies, waits for them, and re-layouts: 3.58 us -> 1.03 us
    ppermute x7, waiting for transfers between devices: 41.3 us -> 33.3 us  [swap(): return lax.ppermute(array, 'bal', [(i, i ^ k) for i in range(bal_size)])]
    all_to_all x1, waiting for transfers between devices: 15.5 us -> 20.5 us  [local(): lax.all_to_all(own_far, ('ctx', 'bal'), split_axis=0, concat_axis=0, tile...]
    pallas_call x1, Pallas kernels: 23.3 us -> 18.5 us  [local(): pl.pallas_call(functools.partial(attend_kernel, per_step, blocks, count,...]
    pallas_call x1, Pallas kernels: 22.8 us -> 26.3 us  [attend_relaid(): pl.pallas_call(functools.partial(attend_kernel, per_step, blocks, count,...]
    unnamed x20 -> x14, local copies, waits for them, and re-layouts: 3.58 us -> 1.03 us
    concatenate x4, other arithmetic: 3.47 us -> 5.49 us  [pack(): jnp.concatenate([first, first], axis=-1)]
    concatenate x4, other arithmetic: 3.39 us -> 5.37 us  [pack(): jnp.concatenate([-second, second], axis=-1)]
  transfers between devices with their start and end apart: 9 -> 9, of which waited for: 4 -> 3; matrix products, arithmetic and copies ran while one was open for 8% -> 11% of each run, Pallas kernels for 35% -> 35%
where the time goes in v1:
time: 163 us; the launch traced here: 162 us
  Pallas kernels  66.3 us (41%)
  waiting for transfers between devices  53.8 us (33%)
  starting transfers between devices  21.2 us (13%)
  other arithmetic  19.3 us (12%)
    ppermute x7, waiting for transfers between devices, swap(): return lax.ppermute(array, 'bal', [(i, i ^ k) for i in range(bal_size)])  33.3 us
    pallas_call x1, Pallas kernels, attend_relaid(): pl.pallas_call(functools.partial(attend_kernel, per_step, blocks, count,...  26.3 us
    all_to_all x1, waiting for transfers between devices, local(): lax.all_to_all(own_far, ('ctx', 'bal'), split_axis=0, concat_axis=0, tile...  20.5 us
    pallas_call x1, Pallas kernels, local(): pl.pallas_call(functools.partial(attend_kernel, per_step, blocks, count,...  18.5 us
    ppermute x7, starting transfers between devices, swap(): return lax.ppermute(array, 'bal', [(i, i ^ k) for i in range(bal_size)])  9.43 us
    pallas_call x1, Pallas kernels, local(): pl.pallas_call(functools.partial(patch_kernel, heads, blocks, edge), in_s...  6.75 us
    pallas_call x2, Pallas kernels, send_inputs(): pl.pallas_call(functools.partial(pack_kernel, jobs), in_specs=[smem] + [a...  6.45 us
    all_to_all x1, starting transfers between devices, local(): lax.all_to_all(own_far, ('ctx', 'bal'), split_axis=0, concat_axis=0, tile...  5.95 us
  transfers between devices with their start and end apart: 9, of which 3 were waited for; matrix products, arithmetic and copies ran while one was open for 11% of the time, Pallas kernels for 35%

profile of v1, /device:TPU:0, one launch (start us, length us, event | category | flops | bytes accessed | tf_op | source)
XLA Modules:
  0.0 162.4 jit_solution(2865457018167321886)
XLA Ops:
  0.6 0.7 and_select_fusion.9
  1.6 0.7 pad_add_fusion.2.info
  2.2 3.0 %shard_map.102.after = bf16[4,128,1536]{2,1,0:T(8,128)(2,1)} custom-call(s32[8]{0:T(128)} %pad_add_fusion.2.info, s32[128]{0:T(128)} %after.1, bf16[512,2560]{1,0:T(8,128)(2,1)} %rest_4_.3, bf16[512,2560]{1,0:T(8,128)(2,1)} %rest_5_.3, bf16[512,2560]{1,0:T(8,128)(2,1)} %rest_6_.3, bf16[512,2560]{1,0:T(8,128)(2,1)} %rest_7_.3), custom_call_target="tpu_custom_call" | custom-call | tf_op jit(solution)/shard_map/pallas_call | solution.py:357
  5.2 3.0 %collective-permute-start.2 = (bf16[4,128,1536]{2,1,0:T(8,128)(2,1)}, bf16[4,128,1536]{2,1,0:T(8,128)(2,1)}, u32[]{:S(2)}, u32[]{:S(2)}) collective-permute-start(bf16[4,128,1536]{2,1,0:T(8,128)(2,1)} %shard_map.102.after), channel_id=1, source_target_pairs={{0,2},{1,3},{2,0},{3,1},{4,6},{5,7},{6,4},{7,5},{8,10},{9,11},{10,... | collective-permute-start | bytes 4718600 | tf_op jit(solution)/shard_map/ppermute | solution.py:335
  8.7 1.3 fusion.17
  10.0 4.7 %shard_map.103.after = bf16[16,8,2560]{2,1,0:T(8,128)(2,1)} custom-call(s32[20]{0:T(128)} %phase.7, bf16[512,2560]{1,0:T(8,128)(2,1)} %rest_5_.3, bf16[512,2560]{1,0:T(8,128)(2,1)} %rest_6_.3, f32[4,2560]{1,0:T(4,128)} %get-tuple-element.42.cos_ref, f32[4,2560]{1,0:T(4,128)} %get-tuple-element.43.sin_ref, bf16[4,128,1536]{2,1,0:T(8,128)(2,1)} %shard_map.102.after), custom_call_target="tpu_custom_call" | custom-call | tf_op jit(solution)/shard_map/pallas_call | solution.py:373
  14.7 6.0 %all-to-all-start = ((bf16[16,8,2560]{2,1,0:T(8,128)(2,1)}), bf16[16,8,2560]{2,1,0:T(8,128)(2,1)S(1)}, u32[]{:S(2)}, u32[]{:S(2)}) async-start(bf16[16,8,2560]{2,1,0:T(8,128)(2,1)} %shard_map.103.after), calls=%async_computation | async-start | bytes 1310720 | tf_op jit(solution)/shard_map/all_to_all | solution.py:395
  20.6 3.5 %shard_map.104 = (bf16[4,128,1536]{2,1,0:T(8,128)(2,1)}, bf16[4,128,1536]{2,1,0:T(8,128)(2,1)}) custom-call(s32[8]{0:T(128)} %pad_add_fusion.2.info, bf16[16,8,2560]{2,1,0:T(8,128)(2,1)} %shard_map.103.after, bf16[512,2560]{1,0:T(8,128)(2,1)} %rest_4_.3, bf16[512,2560]{1,0:T(8,128)(2,1)} %rest_5_.3, bf16[512,2560]{1,0:T(8,128)(2,1)} %rest_6_.3, ...), custom_call_target="tpu_custom_call" | custom-call | tf_op jit(solution)/shard_map/pallas_call | solution.py:357
  24.2 2.0 %collective-permute-start.3 = (bf16[4,128,1536]{2,1,0:T(8,128)(2,1)}, bf16[4,128,1536]{2,1,0:T(8,128)(2,1)}, u32[]{:S(2)}, u32[]{:S(2)}) collective-permute-start(bf16[4,128,1536]{2,1,0:T(8,128)(2,1)} %get-tuple-element.21), channel_id=1, source_target_pairs={{0,3},{1,2},{2,1},{3,0},{4,7},{5,6},{6,5},{7,4},{8,11},{9,10},{10,... | collective-permute-start | bytes 4718600 | tf_op jit(solution)/shard_map/ppermute | solution.py:335
  26.8 3.3 %fusion.13 = (f32[512,64]{1,0:T(8,128)S(1)}, f32[512,64]{1,0:T(8,128)S(1)}, f32[512,64]{1,0:T(8,128)S(1)}, f32[512,64]{1,0:T(8,128)S(1)}, f32[512,64]{1,0:T(8,12...) fusion(f32[64]{0:T(128)S(1)} %get-tuple-element.72, ...), kind=kLoop, calls=%fused_computation.31 | loop fusion | flops 589824 | bytes 1581568 | tf_op jit(solution)/shard_map/neg | solution.py:32
  30.0 0.8 pad_maximum_fusion.4.rest_0_
  30.9 20.5 %all-to-all-done = bf16[16,8,2560]{2,1,0:T(8,128)(2,1)S(1)} async-done(((bf16[16,8,2560]{2,1,0:T(8,128)(2,1)}), bf16[16,8,2560]{2,1,0:T(8,128)(2,1)S(1)}, u32[]{:S(2)}, u32[]{:S(2)}) %all-to-all-start) | async-done | bytes 655392 | tf_op jit(solution)/shard_map/all_to_all | solution.py:395
  51.4 0.9 pad_maximum_fusion.6.rest_2_
  52.3 0.9 pad_maximum_fusion.7.rest_3_
  53.1 0.8 pad_maximum_fusion.5.rest_1_
  54.0 0.8 fusion.10
  54.7 0.9 copy-done.1
  55.6 18.5 %shard_map.105 = (bf16[4,128,1024]{2,1,0:T(8,128)(2,1)}, bf16[4,128,1024]{2,1,0:T(8,128)(2,1)}, bf16[4,128,1024]{2,1,0:T(8,128)(2,1)}, bf16[4,128,1024]{2,1,0:T(8,128)(2,1)}, bf16[256,2560]{1,0:T(8,128)(2,1)}) custom-call(s32[8]{0:T(128)} %pad_add_fusion.2.info, s32[20]{0:T(128)} %phase.7, s32[20]{0:T(128)} %seg.3, bf16[128,2560]{1,0:T(8,128)(2,1)} %bitcast.58, ...), custom_call_target="tpu_custom_call" | custom-call | flops 20000000000 | bytes 60000000 | tf_op jit(solution)/shard_map/pallas_call | solution.py:430
  74.1 2.4 %collective-permute-start.4 = (bf16[4,128,1024]{2,1,0:T(8,128)(2,1)}, bf16[4,128,1024]{2,1,0:T(8,128)(2,1)}, u32[]{:S(2)}, u32[]{:S(2)}) collective-permute-start(bf16[4,128,1024]{2,1,0:T(8,128)(2,1)} %get-tuple-element.24), channel_id=1, source_target_pairs={{0,2},{1,3},{2,0},{3,1},{4,6},{5,7},{6,4},{7,5},{8,10},{9,11},{10,... | collective-permute-start | bytes 3145736 | tf_op jit(solution)/shard_map/ppermute | solution.py:335
  76.6 0.7 pad_add_fusion.1.info
  77.2 1.9 %pad_maximum_fusion.rest_0_ = f32[512,128]{1,0:T(8,128)} fusion(f32[512,64]{1,0:T(8,128)} %get-tuple-element.56), kind=kLoop, calls=%fused_computation.12 | loop fusion | flops 65536 | bytes 393216 | tf_op jit(solution)/shard_map/concatenate | solution.py:31
  79.1 1.9 %pad_maximum_fusion.2.rest_2_ = f32[512,128]{1,0:T(8,128)} fusion(f32[512,64]{1,0:T(8,128)} %get-tuple-element.59), kind=kLoop, calls=%fused_computation.14 | loop fusion | flops 65536 | bytes 393216 | tf_op jit(solution)/shard_map/concatenate | solution.py:31
  80.9 1.9 %pad_maximum_fusion.3.rest_3_ = f32[512,128]{1,0:T(8,128)} fusion(f32[512,64]{1,0:T(8,128)} %get-tuple-element.57, f32[512,64]{1,0:T(8,128)} %get-tuple-element.61), kind=kLoop, calls=%fused_computation.15 | loop fusion | flops 65536 | bytes 524288 | tf_op jit(solution)/shard_map/concatenate | solution.py:32
  82.8 1.8 %pad_maximum_fusion.1.rest_1_ = f32[512,128]{1,0:T(8,128)} fusion(f32[512,64]{1,0:T(8,128)S(1)} %get-tuple-element.58, f32[512,64]{1,0:T(8,128)} %get-tuple-element.60), kind=kLoop, calls=%fused_computation.13 | loop fusion | flops 65536 | bytes 524288 | tf_op jit(solution)/shard_map/concatenate | solution.py:32
  84.6 26.3 %shard_map.106 = (bf16[4,128,2560]{2,1,0:T(8,128)(2,1)}, bf16[4,128,2560]{2,1,0:T(8,128)(2,1)}, bf16[4,128,2560]{2,1,0:T(8,128)(2,1)}, bf16[4,128,2560]{2,1,0:T(8,128)(2,1)}, bf16[256,2560]{1,0:T(8,128)(2,1)}) custom-call(s32[12]{0:T(128)} %pad_add_fusion.1.info, s32[20]{0:T(128)} %phase.7, s32[20]{0:T(128)} %seg.3, ...), custom_call_target="tpu_custom_call", output_to_operand_aliasing={{4}: (18, {})} | custom-call | flops 2000000000 | bytes 5000000 | tf_op jit(solution)/shard_map/pallas_call | solution.py:477
  111.0 5.8 %all-to-all-start.1 = ((bf16[32,8,2560]{2,1,0:T(8,128)(2,1)}), bf16[32,8,2560]{2,1,0:T(8,128)(2,1)}, u32[]{:S(2)}, u32[]{:S(2)}) async-start(bf16[32,8,2560]{2,1,0:T(8,128)(2,1)} %bitcast.52), calls=%async_computation.1 | async-start | bytes 2621440 | tf_op jit(solution)/shard_map/all_to_all | solution.py:524
  116.8 0.3 collective-permute-start.6
  117.0 1.6 %collective-permute-start.5 = (bf16[4,128,1024]{2,1,0:T(8,128)(2,1)}, bf16[4,128,1024]{2,1,0:T(8,128)(2,1)}, u32[]{:S(2)}, u32[]{:S(2)}) collective-permute-start(bf16[4,128,1024]{2,1,0:T(8,128)(2,1)} %get-tuple-element.25), channel_id=1, source_target_pairs={{0,3},{1,2},{2,1},{3,0},{4,7},{5,6},{6,5},{7,4},{8,11},{9,10},{10,... | collective-permute-start | bytes 3145736 | tf_op jit(solution)/shard_map/ppermute | solution.py:335
  118.7 1.0 collective-permute-done.6.rest_1_
  119.7 3.7 %shard_map.108 = (bf16[512,2560]{1,0:T(8,128)(2,1)}, bf16[512,2560]{1,0:T(8,128)(2,1)}, bf16[512,2560]{1,0:T(8,128)(2,1)}, bf16[512,2560]{1,0:T(8,128)(2,1)}) custom-call(s32[4]{0:T(128)} %copy-done.2, bf16[4,128,1024]{2,1,0:T(8,128)(2,1)} %get-tuple-element.26.rest_0_, ...), custom_call_target="tpu_custom_call", output_to_operand_aliasing={{0}: (4, {}), {1}: (5, {}), {2}: (6, {}), {3}: (7, {})} | custom-call | flops 2000000000 | bytes 5000000 | tf_op jit(solution)/shard_map/pallas_call | solution.py:537
  123.3 32.3 %collective-permute-done.5.part = bf16[4,128,1024]{2,1,0:T(8,128)(2,1)} collective-permute-done((bf16[4,128,1024]{2,1,0:T(8,128)(2,1)}, bf16[4,128,1024]{2,1,0:T(8,128)(2,1)}, u32[]{:S(2)}, u32[]{:S(2)}) %collective-permute-start.5) | collective-permute-done | bytes 1048608 | tf_op jit(solution)/shard_map/ppermute | solution.py:335
  155.7 6.8 %shard_map.109 = (bf16[512,2560]{1,0:T(8,128)(2,1)}, bf16[512,2560]{1,0:T(8,128)(2,1)}, bf16[512,2560]{1,0:T(8,128)(2,1)}, bf16[512,2560]{1,0:T(8,128)(2,1)}) custom-call(s32[20]{0:T(128)} %phase.7, s32[4]{0:T(128)} %copy-done.2, ...), custom_call_target="tpu_custom_call", output_to_operand_aliasing={{0}: (6, {}), {1}: (7, {}), {2}: (8, {}), {3}: (9, {})} | custom-call | tf_op jit(solution)/shard_map/pallas_call | solution.py:552
  (41 shorter events, 1.3 us)
Async XLA Ops:
  1.4 75.2 %copy-start.2 = (s32[4]{0:T(128)}, s32[4]{0:T(128)S(1)}, u32[]{:S(2)}) copy-start(s32[4]{0:T(128)S(1)} %get-tuple-element.69.slot) | copy-start | bytes 52
  2.2 6.0 %copy-start.4 = (s32[128]{0:T(128)S(1)}, s32[128]{0:T(128)}, u32[]{:S(2)}) copy-start(s32[128]{0:T(128)} %after.1) | copy-start | bytes 1540
  2.2 6.3 %copy-start.3 = (s32[20]{0:T(128)S(1)}, s32[20]{0:T(128)}, u32[]{:S(2)}) copy-start(s32[20]{0:T(128)} %phase.7) | copy-start | bytes 244
  5.2 79.4 %collective-permute-start.2 = (bf16[4,128,1536]{2,1,0:T(8,128)(2,1)}, bf16[4,128,1536]{2,1,0:T(8,128)(2,1)}, u32[]{:S(2)}, u32[]{:S(2)}) collective-permute-start(bf16[4,128,1536]{2,1,0:T(8,128)(2,1)} %shard_map.102.after), channel_id=1, source_target_pairs={{0,2},{1,3},{2,0},{3,1},{4,6},{5,7},{6,4},{7,5},{8,10},{9,11},{10,... | collective-permute-start | bytes 4718600 | tf_op jit(solution)/shard_map/ppermute | solution.py:335
  14.7 36.7 %all-to-all-start = ((bf16[16,8,2560]{2,1,0:T(8,128)(2,1)}), bf16[16,8,2560]{2,1,0:T(8,128)(2,1)S(1)}, u32[]{:S(2)}, u32[]{:S(2)}) async-start(bf16[16,8,2560]{2,1,0:T(8,128)(2,1)} %shard_map.103.after), calls=%async_computation | async-start | bytes 1310720 | tf_op jit(solution)/shard_map/all_to_all | solution.py:395
  24.1 60.5 %collective-permute-start.1 = (bf16[4,128,1536]{2,1,0:T(8,128)(2,1)}, bf16[4,128,1536]{2,1,0:T(8,128)(2,1)}, u32[]{:S(2)}, u32[]{:S(2)}) collective-permute-start(bf16[4,128,1536]{2,1,0:T(8,128)(2,1)} %get-tuple-element.20), channel_id=1, source_target_pairs={{0,1},{1,0},{2,3},{3,2},{4,5},{5,4},{6,7},{7,6},{8,9},{9,8},{10,11... | collective-permute-start | bytes 4718600 | tf_op jit(solution)/shard_map/ppermute | solution.py:335
  24.2 60.4 %collective-permute-start.3 = (bf16[4,128,1536]{2,1,0:T(8,128)(2,1)}, bf16[4,128,1536]{2,1,0:T(8,128)(2,1)}, u32[]{:S(2)}, u32[]{:S(2)}) collective-permute-start(bf16[4,128,1536]{2,1,0:T(8,128)(2,1)} %get-tuple-element.21), channel_id=1, source_target_pairs={{0,3},{1,2},{2,1},{3,0},{4,7},{5,6},{6,5},{7,4},{8,11},{9,10},{10,... | collective-permute-start | bytes 4718600 | tf_op jit(solution)/shard_map/ppermute | solution.py:335
  51.3 4.3 %copy-start = (bf16[16,8,2560]{2,1,0:T(8,128)(2,1)}, bf16[16,8,2560]{2,1,0:T(8,128)(2,1)S(1)}, u32[]{:S(2)}) copy-start(bf16[16,8,2560]{2,1,0:T(8,128)(2,1)S(1)} %all-to-all-done) | copy-start | bytes 1966084
  51.3 3.4 %collective-permute-start = (bf16[128,2560]{1,0:T(8,128)(2,1)S(1)}, bf16[128,2560]{1,0:T(8,128)(2,1)S(1)}, u32[]{:S(2)}, u32[]{:S(2)}) collective-permute-start(bf16[128,2560]{1,0:T(8,128)(2,1)S(1)} %bitcast.57), channel_id=1, source_target_pairs={{0,1},{1,0},{2,3},{3,2},{4,5},{5,4},{6,7},{7,6},{8,9},{9,8},{10,11... | collective-permute-start | bytes 1966088 | tf_op jit(solution)/shard_map/ppermute | solution.py:335
  54.7 0.9 copy-start.1
  74.1 36.8 %collective-permute-start.4 = (bf16[4,128,1024]{2,1,0:T(8,128)(2,1)}, bf16[4,128,1024]{2,1,0:T(8,128)(2,1)}, u32[]{:S(2)}, u32[]{:S(2)}) collective-permute-start(bf16[4,128,1024]{2,1,0:T(8,128)(2,1)} %get-tuple-element.24), channel_id=1, source_target_pairs={{0,2},{1,3},{2,0},{3,1},{4,6},{5,7},{6,4},{7,5},{8,10},{9,11},{10,... | collective-permute-start | bytes 3145736 | tf_op jit(solution)/shard_map/ppermute | solution.py:335
  110.9 5.8 %copy-start.5 = (bf16[4,128,1024]{2,1,0:T(8,128)(2,1)S(1)}, bf16[4,128,1024]{2,1,0:T(8,128)(2,1)}, u32[]{:S(2)}) copy-start(bf16[4,128,1024]{2,1,0:T(8,128)(2,1)} %get-tuple-element.27) | copy-start | bytes 3145732
  111.0 44.7 %all-to-all-start.1 = ((bf16[32,8,2560]{2,1,0:T(8,128)(2,1)}), bf16[32,8,2560]{2,1,0:T(8,128)(2,1)}, u32[]{:S(2)}, u32[]{:S(2)}) async-start(bf16[32,8,2560]{2,1,0:T(8,128)(2,1)} %bitcast.52), calls=%async_computation.1 | async-start | bytes 2621440 | tf_op jit(solution)/shard_map/all_to_all | solution.py:524
  116.8 2.9 %collective-permute-start.6 = (bf16[4,128,1024]{2,1,0:T(8,128)(2,1)S(1)}, bf16[4,128,1024]{2,1,0:T(8,128)(2,1)}, u32[]{:S(2)}, u32[]{:S(2)}) collective-permute-start(bf16[4,128,1024]{2,1,0:T(8,128)(2,1)S(1)} %copy-done.5), channel_id=1, source_target_pairs={{0,1},{1,0},{2,3},{3,2},{4,5},{5,4},{6,7},{7,6},{8,9},{9,8},{10,11... | collective-permute-start | bytes 3145736 | tf_op jit(solution)/shard_map/ppermute | solution.py:335
  117.0 38.6 %collective-permute-start.5 = (bf16[4,128,1024]{2,1,0:T(8,128)(2,1)}, bf16[4,128,1024]{2,1,0:T(8,128)(2,1)}, u32[]{:S(2)}, u32[]{:S(2)}) collective-permute-start(bf16[4,128,1024]{2,1,0:T(8,128)(2,1)} %get-tuple-element.25), channel_id=1, source_target_pairs={{0,3},{1,2},{2,1},{3,0},{4,7},{5,6},{6,5},{7,4},{8,11},{9,10},{10,... | collective-permute-start | bytes 3145736 | tf_op jit(solution)/shard_map/ppermute | solution.py:335

commit v2 on v1

--- a/solution.py
+++ b/solution.py
@@ -55,7 +55,7 @@
 
 
 def attend_kernel(
-    per_step, blocks, count, first, relaid, info, phase, seg, far_ref, other_ref, pull_ref, push_ref, *rest
+    per_step, blocks, count, first, relaid, waits, info, phase, seg, far_ref, other_ref, pull_ref, push_ref, *rest
 ):
     cq_ref, sq_ref, ck_ref, sk_ref = rest[:4]
     own = rest[4:8]
@@ -64,7 +64,7 @@
         come, rest = rest[: blocks - 1], rest[blocks - 1 + relaid :]
         finals, rest = rest[:4], rest[4:]
     else:
-        finals, rest = rest[:blocks], rest[blocks:]
+        finals, rest = rest[waits : waits + blocks], rest[waits + blocks :]
     (pay_ref,) = rest
     scale = 1.0 / math.sqrt(HEAD)
     key_at = lax.broadcasted_iota(jnp.int32, (BLOCK, BLOCK), 0)
@@ -208,105 +208,125 @@
     pass
 
 
-def place_kernel(number, edge, slot, *rest):
+def place_kernel(items, slot, *rest):
+    number = len(items)
     parts = rest[:number]
     finals = rest[number + 4 : number + 8]
-    room, load, save = rest[number + 8 :]
-    width = room.shape[-1]
-
-    def save_of(k, t):
-        start = pl.multiple_of(slot[k] * BLOCK, BLOCK)
-        where = finals[t].at[pl.ds(start, BLOCK), pl.ds(edge, width)]
-        return pltpu.make_async_copy(room.at[k, t], where, save.at[k, t])
-
-    loads = [pltpu.make_async_copy(parts[k], room.at[k], load.at[k]) for k in range(number)]
+    rooms, (load, save) = rest[number + 8 : 2 * number + 8], rest[2 * number + 8 :]
+
+    def save_of(i, t):
+        k, start, width = items[i]
+        top = pl.multiple_of(slot[k] * BLOCK, BLOCK)
+        where = finals[t].at[pl.ds(top, BLOCK), pl.ds(start, width)]
+        return pltpu.make_async_copy(rooms[i].at[t], where, save.at[i, t])
+
+    loads = [pltpu.make_async_copy(parts[i], rooms[i], load.at[i]) for i in range(number)]
     for move in loads:
         move.start()
-    for k in range(number):
-        loads[k].wait()
+    for i in range(number):
+        loads[i].wait()
         for t in range(4):
-            save_of(k, t).start()
-    for k in range(number):
+            save_of(i, t).start()
+    for i in range(number):
         for t in range(4):
-            save_of(k, t).wait()
-
-
-def patch_kernel(
-    heads, blocks, edge, phase, slot, got_hbm, cos_ref, sin_ref, part, *rest
-):
-    outs = rest[4:8]
-    got, room, side, get, load, save, side_load, side_save = rest[8:]
-    width = room.shape[-1]
-    final = blocks - 1
-
-    def rows(k):
-        return pl.ds(pl.multiple_of(slot[k] * BLOCK, BLOCK), BLOCK)
-
-    def left(ref, k):
-        return ref.at[:, pl.ds(0, edge if k == final else width)]
-
-    def store(t, k):
-        return pltpu.make_async_copy(room.at[t, k], outs[2 + t].at[rows(k)], save.at[t, k])
-
-    order = [(k, t) for k in range(blocks) for t in range(2)]
-    fetch = pltpu.make_async_copy(got_hbm, got, get)
-    loads = [
-        pltpu.make_async_copy(
-            left(outs[2 + t].at[rows(k)], k), left(room.at[t, k], k), load.at[t, k]
-        )
-        for k, t in order
-    ]
-    right = pl.ds(edge, width - edge)
-    side_loads = [pltpu.make_async_copy(part.at[t], side.at[t], side_load.at[t]) for t in range(2)]
-    side_loads += [
-        pltpu.make_async_copy(part.at[2 + t], room.at[t, final].at[:, right], side_load.at[2 + t])
-        for t in range(2)
-    ]
-    side_saves = [
-        pltpu.make_async_copy(side.at[t], outs[t].at[rows(final), right], side_save.at[t])
-        for t in range(2)
-    ]
-    fetch.start()
-    for move in loads + side_loads:
-        move.start()
-    fetch.wait()
+            save_of(i, t).wait()
+
+
+def far_rows(got, cos_ref, sin_ref, blocks):
     total = got[0].astype(jnp.float32)
     for sender in range(1, got.shape[0]):
         total = total + got[sender].astype(jnp.float32)
-    got_sum = total
-    spot = lax.broadcasted_iota(jnp.int32, (16, HEAD), 0)
-    line = lax.broadcasted_iota(jnp.int32, (2 * blocks, HEAD), 0)
+    far_k, far_v = total[:blocks], total[blocks:]
+    heads = far_k.shape[1] // HEAD
     turned = []
     for head in range(heads):
         lanes = slice(head * HEAD, (head + 1) * HEAD)
-        far_k = got_sum[:blocks, lanes]
+        one = far_k[:, lanes]
         turned.append(
-            far_k * cos_ref[:, lanes] - pltpu.roll(far_k, HEAD // 2, 1) * sin_ref[:, lanes]
+            one * cos_ref[:, lanes] - pltpu.roll(one, HEAD // 2, 1) * sin_ref[:, lanes]
         )
-    for t in range(2):
-        side_loads[t].wait()
-        side_saves[t].start()
-    for index, (k, t) in enumerate(order):
-        loads[index].wait()
-        if k == final:
-            side_loads[2 + t].wait()
-        for head in range(heads):
-            at = phase[head]
-            start = pl.multiple_of(at // 16 * 16, 16)
+    values = [far_v[:, head * HEAD : (head + 1) * HEAD] for head in range(heads)]
+    return turned, values
+
+
+def overwrite(ref, lanes, at, source, pick):
+    spot = lax.broadcasted_iota(jnp.int32, (16, HEAD), 0)
+    line = lax.broadcasted_iota(jnp.int32, source.shape, 0)
+    start = pl.multiple_of(at // 16 * 16, 16)
+    row = jnp.sum(jnp.where(line == pick, source, 0.0), axis=0, keepdims=True)
+    old = ref[pl.ds(start, 16), lanes].astype(jnp.float32)
+    ref[pl.ds(start, 16), lanes] = jnp.where(spot == at - start, row, old).astype(jnp.bfloat16)
+
+
+def patch_kernel(
+    heads, blocks, late, edge, phase, slot, got_hbm, cos_ref, sin_ref, dk_in, dv_in, dk, dv, got,
+    room, get, load, save
+):
+    outs = (dk, dv)
+    width = room.shape[-1]
+    order = [(k, t) for k in range(blocks) for t in range(2)]
+
+    def span(k):
+        return pl.ds(0, edge if k in late else width)
+
+    def here(t, k):
+        rows = pl.ds(pl.multiple_of(slot[k] * BLOCK, BLOCK), BLOCK)
+        return outs[t].at[rows, span(k)]
+
+    def fetch(t, k):
+        return pltpu.make_async_copy(here(t, k), room.at[t, k, :, span(k)], load.at[t, k])
+
+    def store(t, k):
+        return pltpu.make_async_copy(room.at[t, k, :, span(k)], here(t, k), save.at[t, k])
+
+    first = pltpu.make_async_copy(got_hbm, got, get)
+    first.start()
+    for k, t in order:
+        fetch(t, k).start()
+    first.wait()
+    fresh = far_rows(got, cos_ref, sin_ref, blocks)
+    for k, t in order:
+        fetch(t, k).wait()
+        for head in range(edge // HEAD if k in late else heads):
             lanes = slice(head * HEAD, (head + 1) * HEAD)
-            old = room[t, k, pl.ds(start, 16), lanes].astype(jnp.float32)
-            source = turned[head] if t == 0 else got_sum[blocks:, lanes]
-            row = jnp.sum(
-                jnp.where(line[:blocks] == slot[k], source, 0.0), axis=0, keepdims=True
-            )
-            room[t, k, pl.ds(start, 16), lanes] = jnp.where(spot == at - start, row, old).astype(
-                jnp.bfloat16
-            )
+            overwrite(room.at[t, k], lanes, phase[head], fresh[t][head], slot[k])
         store(t, k).start()
     for k, t in order:
         store(t, k).wait()
-    for move in side_saves:
-        move.wait()
+
+
+def last_kernel(heads, blocks, late, edge, phase, slot, got_hbm, cos_ref, sin_ref, *rest):
+    number = len(late)
+    parts = rest[:number]
+    outs = rest[number + 4 : number + 8]
+    got, room, get, load, save = rest[number + 8 :]
+    right = pl.ds(edge, room.shape[-1])
+
+    def store(i, t):
+        rows = pl.ds(pl.multiple_of(slot[late[i]] * BLOCK, BLOCK), BLOCK)
+        return pltpu.make_async_copy(room.at[i, t], outs[t].at[rows, right], save.at[i, t])
+
+    first = pltpu.make_async_copy(got_hbm.at[:, :, right], got, get)
+    loads = [pltpu.make_async_copy(parts[i], room.at[i], load.at[i]) for i in range(number)]
+    for move in loads + [first]:
+        move.start()
+    for i in range(number):
+        loads[i].wait()
+        for t in range(2):
+            store(i, t).start()
+    first.wait()
+    fresh = far_rows(got, cos_ref, sin_ref, blocks)
+    for i in range(number):
+        for t in range(2):
+            for head in range(edge // HEAD, heads):
+                local_head = head - edge // HEAD
+                lanes = slice(local_head * HEAD, (local_head + 1) * HEAD)
+                source = fresh[t][local_head]
+                overwrite(room.at[i, 2 + t], lanes, phase[head], source, slot[late[i]])
+            store(i, 2 + t).start()
+    for i in range(number):
+        for t in range(4):
+            store(i, t).wait()
 
 
 def local(queries, keys, values, output_gradient, dilation_phase, segment_device_count, owner):
@@ -348,8 +368,9 @@
     )
 
     first = heads * 3 // 10 * 2
-    last = heads - first
-    edge = first * HEAD
+    early = first // 4 * 2
+    middle = heads - 2
+    cut, edge, brim = early * HEAD, first * HEAD, middle * HEAD
     originals = (queries, keys, values, output_gradient)
 
     def send_inputs(jobs, after):
@@ -365,7 +386,7 @@
         )(info, after, *originals)
         return sent, [swap(one, job[0]) for one, job in zip(sent, jobs)]
 
-    sent, come_early = send_inputs([(2, 0, edge)], owner)
+    sent, come_early = send_inputs([(2, 0, cut)], owner)
 
     cq, sq, ck, sk = tables(tokens_of(held), total)
     own_phase = (held[:, None] * BLOCK + dilation_phase[None, :]).astype(jnp.int32)
@@ -401,10 +422,17 @@
         axis_index_groups=halves,
     ).reshape(count, width)
     other_far = swap(near_far, 1)
-    later = [3, 1]
-    _, come_late = send_inputs([(k, 0, edge) for k in later], own_far)
-    come = dict(zip([2] + later, come_early + come_late))
-    come = [come[k] for k in range(1, blocks)]
+    jobs = [(2, cut, edge - cut), (3, 0, edge), (1, 0, edge)]
+    _, (come_rest, come_3, come_1) = send_inputs(jobs, own_far)
+    come_2 = come_early[0]
+
+    ids = (device ^ steps) * blocks
+    came = jnp.sum(
+        jnp.where(comes_from[None, :] // blocks * blocks == ids[:, None], comes_from[None, :], 0),
+        axis=1,
+    )
+    moved = jnp.concatenate([which, came, partner]).astype(jnp.int32)
+    moved_tables = tables(tokens_of(came), total)
 
     side = 2 * count
     wide = jnp.arange(side, dtype=jnp.int32)
@@ -423,47 +451,53 @@
     square = pl.BlockSpec((side, side), fixed)
     table = pl.BlockSpec((rows, HEAD), fixed)
     part = pl.BlockSpec((4, BLOCK, columns), lambda h, *_: (0, 0, h))
-    skip = first // per_step
-    tensor = pl.BlockSpec((rows, columns), lambda h, *_: (0, h + skip))
-    lane = pl.BlockSpec((side, columns), lambda h, *_: (0, h + skip))
-    far = pl.BlockSpec((count, columns), lambda h, *_: (0, h + skip))
-    results = pl.pallas_call(
-        functools.partial(attend_kernel, per_step, blocks, count, first, 0),
-        grid_spec=pltpu.PrefetchScalarGridSpec(
-            num_scalar_prefetch=3,
-            grid=(last // per_step,),
-            in_specs=[far, far, square, square] + [table] * 4 + [tensor] * 4,
-            out_specs=[part] * blocks + [lane],
-        ),
-        out_shape=[jax.ShapeDtypeStruct((4, BLOCK, last * HEAD), jnp.bfloat16)] * blocks
-        + [jax.ShapeDtypeStruct((side, width), jnp.bfloat16)],
-        compiler_params=big,
-        cost_estimate=heavy,
-    )(
-        info,
-        dilation_phase,
-        segment_device_count,
-        near_far,
-        other_far,
-        pull,
-        push,
-        cq,
-        sq,
-        ck,
-        sk,
-        *originals,
-    )
-    parts, payload = list(results[:blocks]), results[blocks]
+    def attend_held(begin, end, waits, carried):
+        skip = begin // per_step
+        tensor = pl.BlockSpec((rows, columns), lambda h, *_: (0, h + skip))
+        lane = pl.BlockSpec((side, columns), lambda h, *_: (0, h + skip))
+        far = pl.BlockSpec((count, columns), lambda h, *_: (0, h + skip))
+        extra = carried + waits
+        results = pl.pallas_call(
+            functools.partial(attend_kernel, per_step, blocks, count, begin, 0, len(extra)),
+            grid_spec=pltpu.PrefetchScalarGridSpec(
+                num_scalar_prefetch=3,
+                grid=((end - begin) // per_step,),
+                in_specs=[far, far, square, square]
+                + [table] * 4
+                + [tensor] * 4
+                + [anywhere] * len(extra),
+                out_specs=[part] * blocks + [lane],
+            ),
+            out_shape=[jax.ShapeDtypeStruct((4, BLOCK, (end - begin) * HEAD), jnp.bfloat16)]
+            * blocks
+            + [jax.ShapeDtypeStruct((side, width), jnp.bfloat16)],
+            input_output_aliases={15 + i: blocks for i in range(len(carried))},
+            compiler_params=big,
+            cost_estimate=heavy,
+        )(
+            info,
+            dilation_phase,
+            segment_device_count,
+            near_far,
+            other_far,
+            pull,
+            push,
+            cq,
+            sq,
+            ck,
+            sk,
+            *originals,
+            *extra,
+        )
+        return list(results[:blocks]), results[blocks]
+
+    waits = list(moved_tables) + [come_1, come_2]
+    parts, payload = attend_held(first, middle, waits, [])
+    parts_last, payload = attend_held(middle, heads, [], [payload])
     for k in range(1, blocks):
         parts[k] = swap(parts[k], k)
-
-    ids = (device ^ steps) * blocks
-    came = jnp.sum(
-        jnp.where(comes_from[None, :] // blocks * blocks == ids[:, None], comes_from[None, :], 0),
-        axis=1,
-    )
-    moved = jnp.concatenate([which, came, partner]).astype(jnp.int32)
-    cq, sq, ck, sk = tables(tokens_of(came), total)
+        parts_last[k] = swap(parts_last[k], k)
+
     shapes = [jax.ShapeDtypeStruct((blocks, BLOCK, width), jnp.bfloat16)] * 4
     shapes = shapes + [jax.ShapeDtypeStruct((side, width), jnp.bfloat16)]
 
@@ -473,16 +507,17 @@
         lane = pl.BlockSpec((side, columns), lambda h, *_: (0, h + skip))
         far = pl.BlockSpec((count, columns), lambda h, *_: (0, h + skip))
         whole = pl.BlockSpec((blocks, BLOCK, columns), lambda h, *_: (0, 0, h + skip))
+        shifted = pl.BlockSpec((4, BLOCK, columns), lambda h, *_: (0, 0, h + skip))
         operands = 3 + 4 + 4 + 4 + blocks - 1
         return pl.pallas_call(
-            functools.partial(attend_kernel, per_step, blocks, count, begin, len(carried)),
+            functools.partial(attend_kernel, per_step, blocks, count, begin, len(carried), 0),
             grid_spec=pltpu.PrefetchScalarGridSpec(
                 num_scalar_prefetch=3,
                 grid=((end - begin) // per_step,),
                 in_specs=[far, far, square, square]
                 + [table] * 4
                 + [tensor] * 4
-                + [part] * (blocks - 1)
+                + [shifted, part, shifted]
                 + [anywhere] * len(carried),
                 out_specs=[whole] * 4 + [lane],
                 ),
@@ -500,27 +535,25 @@
             other_far,
             pull,
             push,
-            cq,
-            sq,
-            ck,
-            sk,
+            *moved_tables,
             *originals,
             *come,
             *carried,
         )
 
-    results = attend_relaid(0, first, come, [payload])
+    results = attend_relaid(0, early, [come_1, come_2, come_3], [payload])
+    results = attend_relaid(early, first, [come_1, come_rest, come_3], results)
     finals, payload = [one.reshape(rows, width) for one in results[:4]], results[4]
     payload = pl.pallas_call(
         link_kernel,
-        in_specs=[anywhere, anywhere],
+        in_specs=[anywhere] * 3,
         out_specs=anywhere,
         out_shape=jax.ShapeDtypeStruct((side, width), jnp.bfloat16),
         input_output_aliases={0: 0},
         compiler_params=pltpu.CompilerParams(
             vmem_limit_bytes=room, has_side_effects=True
         ),
-    )(payload, parts[2])
+    )(payload, parts[2], parts[3])
     got = lax.all_to_all(
         payload.reshape(devices, 2 * blocks, width),
         ("ctx", "bal"),
@@ -532,48 +565,63 @@
     new_phase = (comes_from[:, None] * BLOCK + dilation_phase[None, :]).astype(jnp.int32)
     new_cos, new_sin = flat_tables(new_phase, total)
     out = jax.ShapeDtypeStruct((rows, width), jnp.bfloat16)
-    number = blocks - 1
     slots = partner.astype(jnp.int32)
+    items = [(k, edge, brim - edge) for k in range(blocks)]
+    items += [(k, brim, width - brim) for k in range(2)]
+    number = len(items)
     finals = pl.pallas_call(
-        functools.partial(place_kernel, number, edge),
+        functools.partial(place_kernel, items),
         in_specs=[smem] + [anywhere] * (number + 4),
         out_specs=[anywhere] * 4,
         out_shape=[out] * 4,
         input_output_aliases={1 + number + t: t for t in range(4)},
+        scratch_shapes=[pltpu.VMEM((4, BLOCK, item[2]), jnp.bfloat16) for item in items]
+        + [pltpu.SemaphoreType.DMA((number,)), pltpu.SemaphoreType.DMA((number, 4))],
+        compiler_params=big,
+        cost_estimate=light,
+    )(slots, *parts, *parts_last[:2], *finals)
+    late = (2, 3)
+    patched = pl.pallas_call(
+        functools.partial(patch_kernel, heads, blocks, late, brim),
+        in_specs=[smem, smem, anywhere, vmem, vmem, anywhere, anywhere],
+        out_specs=[anywhere] * 2,
+        out_shape=[out] * 2,
+        input_output_aliases={5: 0, 6: 1},
         scratch_shapes=[
-            pltpu.VMEM((number, 4, BLOCK, last * HEAD), jnp.bfloat16),
-            pltpu.SemaphoreType.DMA((number,)),
-            pltpu.SemaphoreType.DMA((number, 4)),
+            pltpu.VMEM((devices, 2 * blocks, width), jnp.bfloat16),
+            pltpu.VMEM((2, blocks, BLOCK, width), jnp.bfloat16),
+            pltpu.SemaphoreType.DMA(()),
+            pltpu.SemaphoreType.DMA((2, blocks)),
+            pltpu.SemaphoreType.DMA((2, blocks)),
         ],
         compiler_params=big,
         cost_estimate=light,
-    )(slots, *parts[:number], *finals)
+    )(dilation_phase, slots, got, new_cos, new_sin, finals[2], finals[3])
     return tuple(
         pl.pallas_call(
-            functools.partial(patch_kernel, heads, blocks, edge),
-            in_specs=[smem, smem, anywhere, vmem, vmem] + [anywhere] * 5,
+            functools.partial(last_kernel, heads, blocks, late, brim),
+            in_specs=[smem, smem, anywhere, vmem, vmem] + [anywhere] * 6,
             out_specs=[anywhere] * 4,
             out_shape=[out] * 4,
-            input_output_aliases={6 + t: t for t in range(4)},
+            input_output_aliases={7 + t: t for t in range(4)},
             scratch_shapes=[
-                pltpu.VMEM((devices, 2 * blocks, width), jnp.bfloat16),
-                pltpu.VMEM((2, blocks, BLOCK, width), jnp.bfloat16),
-                pltpu.VMEM((2, BLOCK, last * HEAD), jnp.bfloat16),
+                pltpu.VMEM((devices, 2 * blocks, width - brim), jnp.bfloat16),
+                pltpu.VMEM((2, 4, BLOCK, width - brim), jnp.bfloat16),
                 pltpu.SemaphoreType.DMA(()),
-                pltpu.SemaphoreType.DMA((2, blocks)),
-                pltpu.SemaphoreType.DMA((2, blocks)),
-                pltpu.SemaphoreType.DMA((4,)),
                 pltpu.SemaphoreType.DMA((2,)),
+                pltpu.SemaphoreType.DMA((2, 4)),
             ],
             compiler_params=big,
         )(
             dilation_phase,
             slots,
             got,
-            new_cos,
-            new_sin,
-            parts[number],
-            *finals,
+            new_cos[:, brim:],
+            new_sin[:, brim:],
+            *parts_last[2:],
+            finals[0],
+            finals[1],
+            *patched,
         )
     )
 

time: 163 us -> 165 us (1.012)
  Pallas kernels: 66.3 us -> 76.2 us
  waiting for transfers between devices: 53.8 us -> 48.2 us
  other arithmetic: 19.3 us -> 13.8 us
  local copies, waits for them, and re-layouts: 1.03 us -> 3.77 us
    all_to_all x1, waiting for transfers between devices: 0.01 us -> 23.3 us  [local(): lax.all_to_all(payload.reshape(devices, 2 * blocks, width), ('ctx', 'bal'...]
    all_to_all x1, waiting for transfers between devices: 20.5 us -> 3.49 us  [local(): lax.all_to_all(own_far, ('ctx', 'bal'), split_axis=0, concat_axis=0, tile...]
    ppermute x7 -> x11, waiting for transfers between devices: 33.3 us -> 21.4 us  [swap(): return lax.ppermute(array, 'bal', [(i, i ^ k) for i in range(bal_size)])]
    pallas_call x4 -> x6, Pallas kernels: 28.9 us -> 34.4 us  [the longest x2 21.7 us: attend_held(): pl.pallas_call(functools.partial(attend_kernel, per_step, blocks, count,...]
    pallas_call x1 -> x2, Pallas kernels: 26.3 us -> 29.8 us  [attend_relaid(): pl.pallas_call(functools.partial(attend_kernel, per_step, blocks, count,...]
    concatenate x4, other arithmetic: 5.49 us -> 3.38 us  [pack(): jnp.concatenate([first, first], axis=-1)]
    concatenate x4, other arithmetic: 5.37 us -> 3.34 us  [pack(): jnp.concatenate([-second, second], axis=-1)]
    ppermute x7 -> x11, starting transfers between devices: 9.43 us -> 9.35 us  [swap(): return lax.ppermute(array, 'bal', [(i, i ^ k) for i in range(bal_size)])]
  transfers between devices with their start and end apart: 9 -> 13, of which waited for: 3 -> 6; matrix products, arithmetic and copies ran while one was open for 11% -> 8% of each run, Pallas kernels for 35% -> 43%
where the time goes in v2:
time: 165 us; the launch traced here: 164 us
  Pallas kernels  76.2 us (46%)
  waiting for transfers between devices  48.2 us (29%)
  starting transfers between devices  20.9 us (13%)
  other arithmetic  13.8 us (8%)
  local copies, waits for them, and re-layouts  3.77 us (2%)
    pallas_call x2, Pallas kernels, attend_relaid(): pl.pallas_call(functools.partial(attend_kernel, per_step, blocks, count,...  29.8 us
    all_to_all x1, waiting for transfers between devices, local(): lax.all_to_all(payload.reshape(devices, 2 * blocks, width), ('ctx', 'bal'...  23.3 us
    pallas_call x2, Pallas kernels, attend_held(): pl.pallas_call(functools.partial(attend_kernel, per_step, blocks, count,...  21.7 us
    ppermute x11, waiting for transfers between devices, swap(): return lax.ppermute(array, 'bal', [(i, i ^ k) for i in range(bal_size)])  21.4 us
    ppermute x11, starting transfers between devices, swap(): return lax.ppermute(array, 'bal', [(i, i ^ k) for i in range(bal_size)])  9.35 us
    pallas_call x2, Pallas kernels, send_inputs(): pl.pallas_call(functools.partial(pack_kernel, jobs), in_specs=[smem] + [a...  7.35 us
    pallas_call x1, Pallas kernels, local(): pl.pallas_call(functools.partial(patch_kernel, heads, blocks, late, brim)...  6.07 us
    all_to_all x1, starting transfers between devices, local(): lax.all_to_all(own_far, ('ctx', 'bal'), split_axis=0, concat_axis=0, tile...  5.95 us
  transfers between devices with their start and end apart: 13, of which 6 were waited for; matrix products, arithmetic and copies ran while one was open for 8% of the time, Pallas kernels for 43%

profile of v2, /device:TPU:0, one launch (start us, length us, event | category | flops | bytes accessed | tf_op | source)
XLA Modules:
  0.0 163.9 jit_solution(16334555994815128816)
XLA Ops:
  2.2 2.8 %shard_map.102.after = bf16[4,128,768]{2,1,0:T(8,128)(2,1)} custom-call(s32[8]{0:T(128)} %pad_add_fusion.2.info, s32[128]{0:T(128)} %after.1, bf16[512,2560]{1,0:T(8,128)(2,1)} %rest_4_.7, bf16[512,2560]{1,0:T(8,128)(2,1)} %rest_5_.7, bf16[512,2560]{1,0:T(8,128)(2,1)} %rest_6_.7, bf16[512,2560]{1,0:T(8,128)(2,1)} %rest_7_.7), custom_call_target="tpu_custom_call" | custom-call | tf_op jit(solution)/shard_map/pallas_call | solution.py:378
  5.0 3.0 %collective-permute-start.4 = (bf16[4,128,768]{2,1,0:T(8,128)(2,1)}, bf16[4,128,768]{2,1,0:T(8,128)(2,1)}, u32[]{:S(2)}, u32[]{:S(2)}) collective-permute-start(bf16[4,128,768]{2,1,0:T(8,128)(2,1)} %shard_map.102.after), channel_id=1, source_target_pairs={{0,2},{1,3},{2,0},{3,1},{4,6},{5,7},{6,4},{7,5},{8,10},{9,11},{10,... | collective-permute-start | bytes 2359304 | tf_op jit(solution)/shard_map/ppermute | solution.py:355
  8.4 1.3 fusion.17
  9.7 4.7 %shard_map.103.after = bf16[16,8,2560]{2,1,0:T(8,128)(2,1)} custom-call(s32[20]{0:T(128)} %phase.13, bf16[512,2560]{1,0:T(8,128)(2,1)} %rest_5_.7, bf16[512,2560]{1,0:T(8,128)(2,1)} %rest_6_.7, f32[4,2560]{1,0:T(4,128)} %get-tuple-element.68.cos_ref, f32[4,2560]{1,0:T(4,128)} %get-tuple-element.69.sin_ref, bf16[4,128,768]{2,1,0:T(8,128)(2,1)} %shard_map.102.after), custom_call_target="tpu_custom_call" | custom-call | tf_op jit(solution)/shard_map/pallas_call | solution.py:394
  14.4 6.0 %all-to-all-start = ((bf16[16,8,2560]{2,1,0:T(8,128)(2,1)}), bf16[16,8,2560]{2,1,0:T(8,128)(2,1)S(1)}, u32[]{:S(2)}, u32[]{:S(2)}) async-start(bf16[16,8,2560]{2,1,0:T(8,128)(2,1)} %shard_map.103.after), calls=%async_computation | async-start | bytes 1310720 | tf_op jit(solution)/shard_map/all_to_all | solution.py:416
  20.4 4.6 %shard_map.104 = (bf16[4,128,768]{2,1,0:T(8,128)(2,1)}, bf16[4,128,1536]{2,1,0:T(8,128)(2,1)}, bf16[4,128,1536]{2,1,0:T(8,128)(2,1)}) custom-call(s32[8]{0:T(128)} %pad_add_fusion.2.info, bf16[16,8,2560]{2,1,0:T(8,128)(2,1)} %shard_map.103.after, bf16[512,2560]{1,0:T(8,128)(2,1)} %rest_4_.7, bf16[512,2560]{1,0:T(8,128)(2,1)} %rest_5_.7, ...), custom_call_target="tpu_custom_call" | custom-call | tf_op jit(solution)/shard_map/pallas_call | solution.py:378
  25.1 2.0 %collective-permute-start.3 = (bf16[4,128,1536]{2,1,0:T(8,128)(2,1)}, bf16[4,128,1536]{2,1,0:T(8,128)(2,1)}, u32[]{:S(2)}, u32[]{:S(2)}) collective-permute-start(bf16[4,128,1536]{2,1,0:T(8,128)(2,1)} %get-tuple-element.35), channel_id=1, source_target_pairs={{0,3},{1,2},{2,1},{3,0},{4,7},{5,6},{6,5},{7,4},{8,11},{9,10},{10,... | collective-permute-start | bytes 4718600 | tf_op jit(solution)/shard_map/ppermute | solution.py:355
  27.7 2.1 %fusion.13 = (f32[512,64]{1,0:T(8,128)S(1)}, f32[512,64]{1,0:T(8,128)S(1)}, f32[512,64]{1,0:T(8,128)S(1)}, f32[512,64]{1,0:T(8,128)S(1)}, f32[512,64]{1,0:T(8,12...) fusion(f32[64]{0:T(128)S(1)} %get-tuple-element.98, ...), kind=kLoop, calls=%fused_computation.31 | loop fusion | flops 589824 | bytes 1581568 | tf_op jit(solution)/shard_map/neg | solution.py:32
  29.8 0.9 pad_maximum_fusion.rest_8_.rest_0_
  30.7 0.8 pad_maximum_fusion.2.rest_10_.rest_2_
  31.5 0.8 pad_maximum_fusion.4.rest_0_
  32.3 0.8 pad_maximum_fusion.6.rest_2_
  34.0 3.5 %all-to-all-done = bf16[16,8,2560]{2,1,0:T(8,128)(2,1)S(1)} async-done(((bf16[16,8,2560]{2,1,0:T(8,128)(2,1)}), bf16[16,8,2560]{2,1,0:T(8,128)(2,1)S(1)}, u32[]{:S(2)}, u32[]{:S(2)}) %all-to-all-start) | async-done | bytes 655392 | tf_op jit(solution)/shard_map/all_to_all | solution.py:416
  38.2 0.8 pad_maximum_fusion.5.rest_1_
  39.0 0.8 pad_maximum_fusion.7.rest_3_
  39.9 0.8 pad_maximum_fusion.1.rest_9_.rest_1_
  41.5 0.8 copy-done.2
  42.3 14.8 %shard_map.105 = (bf16[4,128,768]{2,1,0:T(8,128)(2,1)}, bf16[4,128,768]{2,1,0:T(8,128)(2,1)}, bf16[4,128,768]{2,1,0:T(8,128)(2,1)}, bf16[4,128,768]{2,1,0:T(8,128)(2,1)}, bf16[256,2560]{1,0:T(8,128)(2,1)}) custom-call(s32[8]{0:T(128)} %pad_add_fusion.2.info, s32[20]{0:T(128)} %phase.13, s32[20]{0:T(128)} %seg.7, bf16[128,2560]{1,0:T(8,128)(2,1)} %bitcast.58, ...), custom_call_target="tpu_custom_call" | custom-call | flops 20000000000 | bytes 60000000 | tf_op jit(solution)/shard_map/pallas_call | solution.py:460
  57.7 1.2 collective-permute-start.6
  59.0 7.0 %shard_map.106 = (bf16[4,128,256]{2,1,0:T(8,128)(2,1)}, bf16[4,128,256]{2,1,0:T(8,128)(2,1)}, bf16[4,128,256]{2,1,0:T(8,128)(2,1)}, bf16[4,128,256]{2,1,0:T(8,128)(2,1)}, bf16[256,2560]{1,0:T(8,128)(2,1)}) custom-call(s32[8]{0:T(128)} %pad_add_fusion.2.info, s32[20]{0:T(128)} %phase.13, s32[20]{0:T(128)} %seg.7, ...), custom_call_target="tpu_custom_call", output_to_operand_aliasing={{4}: (15, {})} | custom-call | flops 20000000000 | bytes 60000000 | tf_op jit(solution)/shard_map/pallas_call | solution.py:460
  66.6 15.0 %shard_map.107 = (bf16[4,128,2560]{2,1,0:T(8,128)(2,1)}, bf16[4,128,2560]{2,1,0:T(8,128)(2,1)}, bf16[4,128,2560]{2,1,0:T(8,128)(2,1)}, bf16[4,128,2560]{2,1,0:T(8,128)(2,1)}, bf16[256,2560]{1,0:T(8,128)(2,1)}) custom-call(s32[12]{0:T(128)} %pad_add_fusion.1.info, s32[20]{0:T(128)} %phase.13, s32[20]{0:T(128)} %seg.7, ...), custom_call_target="tpu_custom_call", output_to_operand_aliasing={{4}: (18, {})} | custom-call | flops 2000000000 | bytes 5000000 | tf_op jit(solution)/shard_map/pallas_call | solution.py:512
  81.6 2.3 %collective-permute-done.2.rest_9_ = bf16[4,128,768]{2,1,0:T(8,128)(2,1)} collective-permute-done((bf16[4,128,768]{2,1,0:T(8,128)(2,1)}, bf16[4,128,768]{2,1,0:T(8,128)(2,1)}, u32[]{:S(2)}, u32[]{:S(2)}) %collective-permute-start.2) | collective-permute-done | bytes 786464 | tf_op jit(solution)/shard_map/ppermute | solution.py:355
  83.9 14.8 %shard_map.108 = (bf16[4,128,2560]{2,1,0:T(8,128)(2,1)}, bf16[4,128,2560]{2,1,0:T(8,128)(2,1)}, bf16[4,128,2560]{2,1,0:T(8,128)(2,1)}, bf16[4,128,2560]{2,1,0:T(8,128)(2,1)}, bf16[256,2560]{1,0:T(8,128)(2,1)}) custom-call(s32[12]{0:T(128)} %pad_add_fusion.1.info, ...), custom_call_target="tpu_custom_call", output_to_operand_aliasing={{0}: (18, {}), {1}: (19, {}), {2}: (20, {}), {3}: (21, {}),... | custom-call | flops 2000000000 | bytes 5000000 | tf_op jit(solution)/shard_map/pallas_call | solution.py:512
  98.7 1.9 %collective-permute-done.5.refs_1_.rest_2_ = bf16[4,128,768]{2,1,0:T(8,128)(2,1)S(1)} collective-permute-done((bf16[4,128,768]{2,1,0:T(8,128)(2,1)}, bf16[4,128,768]{2,1,0:T(8,128)(2,1)S(1)}, u32[]{:S(2)}, u32[]{:S(2)}) %collective-permute-start.5) | collective-permute-done | bytes 786464 | tf_op jit(solution)/shard_map/ppermute | solution.py:355
  100.6 16.5 %collective-permute-done.6.refs_2_.rest_3_ = bf16[4,128,768]{2,1,0:T(8,128)(2,1)} collective-permute-done((bf16[4,128,768]{2,1,0:T(8,128)(2,1)}, bf16[4,128,768]{2,1,0:T(8,128)(2,1)}, u32[]{:S(2)}, u32[]{:S(2)}) %collective-permute-start.6) | collective-permute-done | bytes 786464 | tf_op jit(solution)/shard_map/ppermute | solution.py:355
  117.2 5.6 %all-to-all-start.1 = ((bf16[32,8,2560]{2,1,0:T(8,128)(2,1)}), bf16[32,8,2560]{2,1,0:T(8,128)(2,1)}, u32[]{:S(2)}, u32[]{:S(2)}) async-start(bf16[32,8,2560]{2,1,0:T(8,128)(2,1)} %bitcast.56), calls=%async_computation.1 | async-start | bytes 2621440 | tf_op jit(solution)/shard_map/all_to_all | solution.py:557
  124.5 1.7 %collective-permute-start.7 = (bf16[4,128,256]{2,1,0:T(8,128)(2,1)}, bf16[4,128,256]{2,1,0:T(8,128)(2,1)}, u32[]{:S(2)}, u32[]{:S(2)}) collective-permute-start(bf16[4,128,256]{2,1,0:T(8,128)(2,1)} %get-tuple-element.46), channel_id=1, source_target_pairs={{0,2},{1,3},{2,0},{3,1},{4,6},{5,7},{6,4},{7,5},{8,10},{9,11},{10,... | collective-permute-start | bytes 786440 | tf_op jit(solution)/shard_map/ppermute | solution.py:355
  127.0 0.9 copy-done.3
  127.8 3.9 %shard_map.110 = (bf16[512,2560]{1,0:T(8,128)(2,1)}, bf16[512,2560]{1,0:T(8,128)(2,1)}, bf16[512,2560]{1,0:T(8,128)(2,1)}, bf16[512,2560]{1,0:T(8,128)(2,1)}) custom-call(s32[4]{0:T(128)} %copy-done.8, bf16[4,128,768]{2,1,0:T(8,128)(2,1)} %get-tuple-element.48.rest_0_, ...), custom_call_target="tpu_custom_call", output_to_operand_aliasing={{0}: (7, {}), {1}: (8, {}), {2}: (9, {}), {3}: (10, {})} | custom-call | flops 2000000000 | bytes 5000000 | tf_op jit(solution)/shard_map/pallas_call | solution.py:572
  131.7 23.3 %all-to-all-done.1.got_hbm = bf16[32,8,2560]{2,1,0:T(8,128)(2,1)} async-done(((bf16[32,8,2560]{2,1,0:T(8,128)(2,1)}), bf16[32,8,2560]{2,1,0:T(8,128)(2,1)}, u32[]{:S(2)}, u32[]{:S(2)}) %all-to-all-start.1) | async-done | bytes 1310752 | tf_op jit(solution)/shard_map/all_to_all | solution.py:557
  155.0 6.1 %shard_map.111 = (bf16[512,2560]{1,0:T(8,128)(2,1)}, bf16[512,2560]{1,0:T(8,128)(2,1)}) custom-call(s32[20]{0:T(128)} %phase.13, s32[4]{0:T(128)} %copy-done.8, bf16[32,8,2560]{2,1,0:T(8,128)(2,1)} %all-to-all-done.1.got_hbm, f32[4,2560]{1,0:T(4,128)} %copy-done.6, f32[4,2560]{1,0:T(4,128)} %copy-done.5, ...), custom_call_target="tpu_custom_call", output_to_operand_aliasing={{0}: (5, {}), {1}: (6, {})} | custom-call | flops 2000000000 | bytes 5000000 | tf_op jit(solution)/shard_map/pallas_call | solution.py:584
  161.1 2.7 %shard_map.112 = (bf16[512,2560]{1,0:T(8,128)(2,1)}, bf16[512,2560]{1,0:T(8,128)(2,1)}, bf16[512,2560]{1,0:T(8,128)(2,1)}, bf16[512,2560]{1,0:T(8,128)(2,1)}) custom-call(s32[20]{0:T(128)} %phase.13, s32[4]{0:T(128)} %copy-done.8, ...), custom_call_target="tpu_custom_call", output_to_operand_aliasing={{0}: (7, {}), {1}: (8, {}), {2}: (9, {}), {3}: (10, {})} | custom-call | tf_op jit(solution)/shard_map/pallas_call | solution.py:601
  (66 shorter events, 8.7 us)
Async XLA Ops:
  1.4 36.2 %copy-start.8 = (s32[4]{0:T(128)}, s32[4]{0:T(128)S(1)}, u32[]{:S(2)}) copy-start(s32[4]{0:T(128)S(1)} %get-tuple-element.95.slot) | copy-start | bytes 52
  2.2 5.8 %copy-start.9 = (s32[128]{0:T(128)S(1)}, s32[128]{0:T(128)}, u32[]{:S(2)}) copy-start(s32[128]{0:T(128)} %after.1) | copy-start | bytes 1540
  2.2 6.0 %copy-start.7 = (s32[20]{0:T(128)S(1)}, s32[20]{0:T(128)}, u32[]{:S(2)}) copy-start(s32[20]{0:T(128)} %phase.13) | copy-start | bytes 244
  5.0 36.5 %collective-permute-start.4 = (bf16[4,128,768]{2,1,0:T(8,128)(2,1)}, bf16[4,128,768]{2,1,0:T(8,128)(2,1)}, u32[]{:S(2)}, u32[]{:S(2)}) collective-permute-start(bf16[4,128,768]{2,1,0:T(8,128)(2,1)} %shard_map.102.after), channel_id=1, source_target_pairs={{0,2},{1,3},{2,0},{3,1},{4,6},{5,7},{6,4},{7,5},{8,10},{9,11},{10,... | collective-permute-start | bytes 2359304 | tf_op jit(solution)/shard_map/ppermute | solution.py:355
  9.7 113.6 %copy-start.6 = (f32[4,2560]{1,0:T(4,128)}, f32[4,2560]{1,0:T(4,128)S(1)}, u32[]{:S(2)}) copy-start(f32[4,2560]{1,0:T(4,128)S(1)} %get-tuple-element.65.cos_ref) | copy-start | bytes 122884
  9.7 114.2 %copy-start.5 = (f32[4,2560]{1,0:T(4,128)}, f32[4,2560]{1,0:T(4,128)S(1)}, u32[]{:S(2)}) copy-start(f32[4,2560]{1,0:T(4,128)S(1)} %get-tuple-element.64.sin_ref) | copy-start | bytes 122884
  14.4 23.1 %all-to-all-start = ((bf16[16,8,2560]{2,1,0:T(8,128)(2,1)}), bf16[16,8,2560]{2,1,0:T(8,128)(2,1)S(1)}, u32[]{:S(2)}, u32[]{:S(2)}) async-start(bf16[16,8,2560]{2,1,0:T(8,128)(2,1)} %shard_map.103.after), calls=%async_computation | async-start | bytes 1310720 | tf_op jit(solution)/shard_map/all_to_all | solution.py:416
  25.0 16.5 %collective-permute-start.1 = (bf16[4,128,1536]{2,1,0:T(8,128)(2,1)}, bf16[4,128,1536]{2,1,0:T(8,128)(2,1)}, u32[]{:S(2)}, u32[]{:S(2)}) collective-permute-start(bf16[4,128,1536]{2,1,0:T(8,128)(2,1)} %get-tuple-element.33), channel_id=1, source_target_pairs={{0,1},{1,0},{2,3},{3,2},{4,5},{5,4},{6,7},{7,6},{8,9},{9,8},{10,11... | collective-permute-start | bytes 4718600 | tf_op jit(solution)/shard_map/ppermute | solution.py:355
  25.1 41.5 %collective-permute-start.3 = (bf16[4,128,1536]{2,1,0:T(8,128)(2,1)}, bf16[4,128,1536]{2,1,0:T(8,128)(2,1)}, u32[]{:S(2)}, u32[]{:S(2)}) collective-permute-start(bf16[4,128,1536]{2,1,0:T(8,128)(2,1)} %get-tuple-element.35), channel_id=1, source_target_pairs={{0,3},{1,2},{2,1},{3,0},{4,7},{5,6},{6,5},{7,4},{8,11},{9,10},{10,... | collective-permute-start | bytes 4718600 | tf_op jit(solution)/shard_map/ppermute | solution.py:355
  27.1 56.8 %collective-permute-start.2 = (bf16[4,128,768]{2,1,0:T(8,128)(2,1)}, bf16[4,128,768]{2,1,0:T(8,128)(2,1)}, u32[]{:S(2)}, u32[]{:S(2)}) collective-permute-start(bf16[4,128,768]{2,1,0:T(8,128)(2,1)} %get-tuple-element.34), channel_id=1, source_target_pairs={{0,2},{1,3},{2,0},{3,1},{4,6},{5,7},{6,4},{7,5},{8,10},{9,11},{10,... | collective-permute-start | bytes 2359304 | tf_op jit(solution)/shard_map/ppermute | solution.py:355
  37.5 4.8 %copy-start = (bf16[16,8,2560]{2,1,0:T(8,128)(2,1)}, bf16[16,8,2560]{2,1,0:T(8,128)(2,1)S(1)}, u32[]{:S(2)}) copy-start(bf16[16,8,2560]{2,1,0:T(8,128)(2,1)S(1)} %all-to-all-done) | copy-start | bytes 1966084
  37.5 3.9 %collective-permute-start = (bf16[128,2560]{1,0:T(8,128)(2,1)S(1)}, bf16[128,2560]{1,0:T(8,128)(2,1)S(1)}, u32[]{:S(2)}, u32[]{:S(2)}) collective-permute-start(bf16[128,2560]{1,0:T(8,128)(2,1)S(1)} %bitcast.57), channel_id=1, source_target_pairs={{0,1},{1,0},{2,3},{3,2},{4,5},{5,4},{6,7},{7,6},{8,9},{9,8},{10,11... | collective-permute-start | bytes 1966088 | tf_op jit(solution)/shard_map/ppermute | solution.py:355
  41.5 0.8 copy-start.2
  57.1 43.5 %collective-permute-start.5 = (bf16[4,128,768]{2,1,0:T(8,128)(2,1)}, bf16[4,128,768]{2,1,0:T(8,128)(2,1)S(1)}, u32[]{:S(2)}, u32[]{:S(2)}) collective-permute-start(bf16[4,128,768]{2,1,0:T(8,128)(2,1)} %get-tuple-element.44), channel_id=1, source_target_pairs={{0,2},{1,3},{2,0},{3,1},{4,6},{5,7},{6,4},{7,5},{8,10},{9,11},{10,... | collective-permute-start | bytes 2359304 | tf_op jit(solution)/shard_map/ppermute | solution.py:355
  57.7 59.4 %collective-permute-start.6 = (bf16[4,128,768]{2,1,0:T(8,128)(2,1)}, bf16[4,128,768]{2,1,0:T(8,128)(2,1)}, u32[]{:S(2)}, u32[]{:S(2)}) collective-permute-start(bf16[4,128,768]{2,1,0:T(8,128)(2,1)} %get-tuple-element.45), channel_id=1, source_target_pairs={{0,3},{1,2},{2,1},{3,0},{4,7},{5,6},{6,5},{7,4},{8,11},{9,10},{10,... | collective-permute-start | bytes 2359304 | tf_op jit(solution)/shard_map/ppermute | solution.py:355
  100.6 16.5 %copy-start.1 = (bf16[4,128,768]{2,1,0:T(8,128)(2,1)}, bf16[4,128,768]{2,1,0:T(8,128)(2,1)S(1)}, u32[]{:S(2)}) copy-start(bf16[4,128,768]{2,1,0:T(8,128)(2,1)S(1)} %collective-permute-done.5.refs_1_.rest_2_) | copy-start | bytes 2359300
  117.1 5.6 %copy-start.10 = (bf16[4,128,768]{2,1,0:T(8,128)(2,1)S(1)}, bf16[4,128,768]{2,1,0:T(8,128)(2,1)}, u32[]{:S(2)}) copy-start(bf16[4,128,768]{2,1,0:T(8,128)(2,1)} %get-tuple-element.49) | copy-start | bytes 2359300
  117.2 5.9 %copy-start.11 = (bf16[4,128,256]{2,1,0:T(8,128)(2,1)S(1)}, bf16[4,128,256]{2,1,0:T(8,128)(2,1)}, u32[]{:S(2)}) copy-start(bf16[4,128,256]{2,1,0:T(8,128)(2,1)} %get-tuple-element.51) | copy-start | bytes 786436
  117.2 37.8 %all-to-all-start.1 = ((bf16[32,8,2560]{2,1,0:T(8,128)(2,1)}), bf16[32,8,2560]{2,1,0:T(8,128)(2,1)}, u32[]{:S(2)}, u32[]{:S(2)}) async-start(bf16[32,8,2560]{2,1,0:T(8,128)(2,1)} %bitcast.56), calls=%async_computation.1 | async-start | bytes 2621440 | tf_op jit(solution)/shard_map/all_to_all | solution.py:557
  122.8 3.5 %collective-permute-start.9 = (bf16[4,128,768]{2,1,0:T(8,128)(2,1)S(1)}, bf16[4,128,768]{2,1,0:T(8,128)(2,1)S(1)}, u32[]{:S(2)}, u32[]{:S(2)}) collective-permute-start(bf16[4,128,768]{2,1,0:T(8,128)(2,1)S(1)} %copy-done.10), channel_id=1, source_target_pairs={{0,1},{1,0},{2,3},{3,2},{4,5},{5,4},{6,7},{7,6},{8,9},{9,8},{10,11... | collective-permute-start | bytes 2359304 | tf_op jit(solution)/shard_map/ppermute | solution.py:355
  123.0 3.2 %collective-permute-start.10 = (bf16[4,128,256]{2,1,0:T(8,128)(2,1)S(1)}, bf16[4,128,256]{2,1,0:T(8,128)(2,1)S(1)}, u32[]{:S(2)}, u32[]{:S(2)}) collective-permute-start(bf16[4,128,256]{2,1,0:T(8,128)(2,1)S(1)} %copy-done.11), channel_id=1, source_target_pairs={{0,1},{1,0},{2,3},{3,2},{4,5},{5,4},{6,7},{7,6},{8,9},{9,8},{10,11... | collective-permute-start | bytes 786440 | tf_op jit(solution)/shard_map/ppermute | solution.py:355
  124.5 36.5 %collective-permute-start.7 = (bf16[4,128,256]{2,1,0:T(8,128)(2,1)}, bf16[4,128,256]{2,1,0:T(8,128)(2,1)}, u32[]{:S(2)}, u32[]{:S(2)}) collective-permute-start(bf16[4,128,256]{2,1,0:T(8,128)(2,1)} %get-tuple-element.46), channel_id=1, source_target_pairs={{0,2},{1,3},{2,0},{3,1},{4,6},{5,7},{6,4},{7,5},{8,10},{9,11},{10,... | collective-permute-start | bytes 786440 | tf_op jit(solution)/shard_map/ppermute | solution.py:355
  126.2 34.8 %collective-permute-start.8 = (bf16[4,128,256]{2,1,0:T(8,128)(2,1)}, bf16[4,128,256]{2,1,0:T(8,128)(2,1)}, u32[]{:S(2)}, u32[]{:S(2)}) collective-permute-start(bf16[4,128,256]{2,1,0:T(8,128)(2,1)} %get-tuple-element.47), channel_id=1, source_target_pairs={{0,3},{1,2},{2,1},{3,0},{4,7},{5,6},{6,5},{7,4},{8,11},{9,10},{10,... | collective-permute-start | bytes 786440 | tf_op jit(solution)/shard_map/ppermute | solution.py:355
  126.3 0.7 copy-start.4
  127.0 0.9 copy-start.3
